TPU v7x, 32 devices: a whole 2x2x4 slice. The times are simulated.
32 devices in a mesh: dp: 4 (over x, core), expert: 8 (over z, y).
Axes of the slice: x: 2, y: 2, z: 4, core: 2. Of those that a mesh axis runs over, the one named last changes fastest.
Arguments:
- tokens: bfloat16 [8192, 768], P(('dp', 'expert')), may hold values from -6 to 6
- segments: int32 [64, 128], P(('dp', 'expert')), may hold values from 0 to 3, never falling along the last dimension, each value on 1 to 64 neighbouring positions
- routes: int32 [8192, 1], P(('dp', 'expert')), may hold values from 0 to 7; in each aligned block of 128 rows (0 to 127, 128 to 255, ...) at most 20 rows name the same one
- qkv_weight: bfloat16 [768, 2304], P(('dp', 'expert')), may hold values from -0.21875 to 0.21875
- out_weight: bfloat16 [768, 768], P(('dp', 'expert')), may hold values from -1.25 to 1.25
- router_weight: bfloat16 [768, 8], P(('dp', 'expert')), may hold values from -0.15625 to 0.15625
- attn_gain: bfloat16 [768], P(('dp', 'expert')), may hold values from 0.5 to 1.5
- moe_gain: bfloat16 [768], P(('dp', 'expert')), may hold values from 0.5 to 1.5
- bias_table: bfloat16 [32, 12], replicated, may hold values from -4 to 4
- up_weight: bfloat16 [8, 768, 3072], P('expert', None, 'dp'), may hold values from -0.21875 to 0.21875
- down_weight: bfloat16 [8, 3072, 768], P('expert', 'dp'), may hold values from -0.875 to 0.875
- cotangent: bfloat16 [8192, 768], P(('dp', 'expert')), may hold values from -6 to 6
Outputs:
- mixed: bfloat16 [8192, 768], P(('dp', 'expert'))
- grad_tokens: float32 [8192, 768], P(('dp', 'expert'))
- grad_qkv: float32 [768, 2304], P(('dp', 'expert'))
- grad_out: float32 [768, 768], P(('dp', 'expert'))
- grad_router: float32 [768, 8], P(('dp', 'expert'))
- grad_attn_gain: float32 [768], P(('dp', 'expert'))
- grad_moe_gain: float32 [768], P(('dp', 'expert'))
- grad_table: float32 [32, 12], replicated
- grad_up: float32 [8, 768, 3072], P('expert', None, 'dp')
- grad_down: float32 [8, 3072, 768], P('expert', 'dp')
Inputs may be any that keep to these rules, and one draw needn't show every extreme that they name: `segments`: each row holds 4 sequences in order, one of them exactly 64 tokens long. `routes`: within the 128 rows of one slab no expert is named more than 20 times, a bound that some block reaches.
All inputs are finite; a program needn't handle non-finite values.
Results may differ from a plain program's by a relative error of at most 0.015.
Values may be sent and summed in bfloat16 or wider, within the bound.
A program may use at most 128 MiB of HBM per device.

v0:
```python
import jax
import jax.numpy as jnp
import numpy as np
from jax import lax
from jax.sharding import PartitionSpec as P

EPS = 1e-06
MASKED = -1e30


def bucket_onehot(length, buckets):
    half_count = buckets // 2
    exact_count = half_count // 2
    offsets = np.arange(length)[None, :] - np.arange(length)[:, None]
    distance = np.abs(offsets)
    scaled = (
        np.log(np.maximum(distance, 1) / exact_count)
        / np.log(128.0 / exact_count)
        * (half_count - exact_count)
    )
    far_bucket = np.minimum(exact_count + np.floor(scaled).astype(np.int32), half_count - 1)
    bucket = np.where(distance < exact_count, distance, far_bucket) + np.where(
        offsets > 0, half_count, 0
    )
    return (bucket[:, :, None] == np.arange(buckets)[None, None, :]).astype(np.float32)


def rms_scale(values, gain_vec):
    return values * lax.rsqrt(jnp.mean(values * values, axis=-1, keepdims=True) + EPS) * gain_vec


def gelu_tanh(values):
    return jax.nn.gelu(values, approximate=True)


def left_dot(left, right):
    return lax.dot_general(
        left, right, (((0,), (0,)), ((), ())), preferred_element_type=jnp.float32
    )


def right_dot(left, right):
    return lax.dot_general(
        left, right, (((1,), (1,)), ((), ())), preferred_element_type=jnp.float32
    )


def gather_dense(qkv_weight, out_weight, router_weight, attn_gain, moe_gain):
    return (
        lax.all_gather(qkv_weight, ("dp", "expert"), axis=0, tiled=True),
        lax.all_gather(out_weight, ("dp", "expert"), axis=0, tiled=True),
        lax.all_gather(router_weight, ("dp", "expert"), axis=0, tiled=True),
        lax.all_gather(attn_gain, ("dp", "expert"), axis=0, tiled=True),
        lax.all_gather(moe_gain, ("dp", "expert"), axis=0, tiled=True),
    )


def score_block(query_rows, key_rows, rel_bias, same_doc, score_scale):
    scores = (
        jnp.einsum("qhd,khd->hqk", query_rows, key_rows, preferred_element_type=jnp.float32)
        * score_scale
    )
    return jnp.where(same_doc[None], scores + rel_bias, MASKED)


def shards(
    tokens,
    segments,
    routes,
    qkv_weight,
    out_weight,
    router_weight,
    attn_gain,
    moe_gain,
    bias_table,
    up_weight,
    down_weight,
    cotangent,
):
    micro_count, length = segments.shape
    model_width = tokens.shape[1]
    buckets, head_count = bias_table.shape
    head_size = model_width // head_count
    score_scale = head_size ** (-0.5)
    experts = router_weight.shape[1]
    capacity = max(2, (5 * length + 4 * experts - 1) // (4 * experts))
    flat_hot = jnp.asarray(bucket_onehot(length, buckets).reshape(length * length, buckets))
    table_bias = jnp.dot(
        flat_hot.astype(jnp.bfloat16), bias_table, preferred_element_type=jnp.float32
    )
    rel_bias = table_bias.reshape(length, length, head_count).transpose(2, 0, 1)
    kept_weights = gather_dense(qkv_weight, out_weight, router_weight, attn_gain, moe_gain)
    up_mat, down_mat = (up_weight[0], down_weight[0])
    acc_gain_one = jnp.zeros((model_width,), jnp.float32)
    acc_gain_two = jnp.zeros((model_width,), jnp.float32)
    acc_table = jnp.zeros((buckets, head_count), jnp.float32)
    normed_one_list, packed_grad_list = ([], [])
    attended_list, branch_list = ([], [])
    normed_two_list, logits_list = ([], [])
    expert_in_list, hidden_grad_list = ([], [])
    act_list, expert_grad_list = ([], [])
    mixed_parts = []
    grad_parts = []
    for micro_index in range(micro_count):
        row_begin = micro_index * length
        inputs = tokens[row_begin : row_begin + length].astype(jnp.float32)
        segment_ids = segments[micro_index]
        same_doc = segment_ids[:, None] == segment_ids[None, :]
        route_ids = routes[row_begin : row_begin + length, 0]
        w_qkv, w_out, w_router, gain_one, gain_two = kept_weights
        gain_one = gain_one.astype(jnp.float32)
        gain_two = gain_two.astype(jnp.float32)
        normed_one = rms_scale(inputs, gain_one).astype(jnp.bfloat16)
        packed = jnp.dot(normed_one, w_qkv, preferred_element_type=jnp.float32).astype(jnp.bfloat16)
        packed = packed.reshape(length, 3, head_count, head_size)
        query_rows, key_rows, value_rows = (packed[:, 0], packed[:, 1], packed[:, 2])
        scores = score_block(query_rows, key_rows, rel_bias, same_doc, score_scale)
        row_max = jnp.max(scores, axis=-1, keepdims=True)
        expo = jnp.exp(scores - row_max)
        row_total = jnp.sum(expo, axis=-1, keepdims=True)
        attn_probs = expo / row_total
        log_total = row_max + jnp.log(row_total)
        attended = jnp.einsum(
            "hqk,khd->qhd",
            attn_probs.astype(jnp.bfloat16),
            value_rows,
            preferred_element_type=jnp.float32,
        )
        attended = attended.astype(jnp.bfloat16).reshape(length, model_width)
        after_attn = inputs + jnp.dot(attended, w_out, preferred_element_type=jnp.float32)
        normed_two = rms_scale(after_attn, gain_two).astype(jnp.bfloat16)
        logits = jnp.dot(normed_two, w_router, preferred_element_type=jnp.float32)
        router_probs = jax.nn.softmax(logits, axis=-1)
        route_hot = (route_ids[:, None] == jnp.arange(experts, dtype=jnp.int32)[None, :]).astype(
            jnp.int32
        )
        slot_index = jnp.sum(route_hot * (jnp.cumsum(route_hot, axis=0) - 1), axis=1)
        position = route_ids * capacity + slot_index
        dispatch = (
            jnp.arange(experts * capacity, dtype=jnp.int32)[:, None] == position[None, :]
        ).astype(jnp.bfloat16)
        hot_float = route_hot.astype(jnp.float32)
        gate_prob = jnp.sum(router_probs * hot_float, axis=1, keepdims=True)
        sent_rows = jnp.dot(dispatch, normed_two, preferred_element_type=jnp.float32).astype(
            jnp.bfloat16
        )
        received = lax.all_to_all(
            sent_rows.reshape(experts, capacity, model_width),
            "expert",
            split_axis=0,
            concat_axis=0,
            tiled=True,
        )
        received = received.reshape(experts * capacity, model_width)
        expert_in = lax.all_gather(received, "dp", axis=0, tiled=True)
        hidden = jnp.dot(expert_in, up_mat, preferred_element_type=jnp.float32)
        act_low = gelu_tanh(hidden).astype(jnp.bfloat16)
        expert_out = lax.psum_scatter(
            jnp.dot(act_low, down_mat, preferred_element_type=jnp.float32).astype(jnp.bfloat16),
            "dp",
            scatter_dimension=0,
            tiled=True,
        )
        expert_low = expert_out.reshape(experts, capacity, model_width)
        returned = lax.all_to_all(
            expert_low, "expert", split_axis=0, concat_axis=0, tiled=True
        ).reshape(experts * capacity, model_width)
        combined = left_dot(dispatch, returned)
        mixed_parts.append((after_attn + gate_prob * combined).astype(jnp.bfloat16))
        w_qkv, w_out, w_router, gain_one, gain_two = kept_weights
        gain_one = gain_one.astype(jnp.float32)
        gain_two = gain_two.astype(jnp.float32)
        upstream = cotangent[row_begin : row_begin + length].astype(jnp.float32)
        grad_gate = jnp.sum(upstream * combined, axis=1, keepdims=True)
        grad_token_out = (gate_prob * upstream).astype(jnp.bfloat16)
        grad_slots = jnp.dot(dispatch, grad_token_out, preferred_element_type=jnp.float32).astype(
            jnp.bfloat16
        )
        grad_back = lax.all_to_all(
            grad_slots.reshape(experts, capacity, model_width),
            "expert",
            split_axis=0,
            concat_axis=0,
            tiled=True,
        )
        grad_back = grad_back.reshape(experts * capacity, model_width)
        grad_expert_out = lax.all_gather(grad_back, "dp", axis=0, tiled=True)
        grad_activation = right_dot(grad_expert_out, down_mat)
        grad_hidden = jax.vjp(gelu_tanh, hidden)[1](grad_activation)[0].astype(jnp.bfloat16)
        act_list.append(act_low)
        expert_grad_list.append(grad_expert_out)
        expert_in_list.append(expert_in)
        hidden_grad_list.append(grad_hidden)
        grad_dispatched = lax.psum_scatter(
            right_dot(grad_hidden, up_mat).astype(jnp.bfloat16),
            "dp",
            scatter_dimension=0,
            tiled=True,
        ).astype(jnp.float32)
        grad_dispatched = grad_dispatched.astype(jnp.bfloat16).reshape(
            experts, capacity, model_width
        )
        grad_arrived = lax.all_to_all(
            grad_dispatched, "expert", split_axis=0, concat_axis=0, tiled=True
        ).reshape(experts * capacity, model_width)
        grad_normed_two = left_dot(dispatch, grad_arrived)
        grad_logits = (router_probs * (hot_float - gate_prob) * grad_gate).astype(jnp.bfloat16)
        normed_two_list.append(normed_two)
        logits_list.append(grad_logits)
        grad_normed_two = grad_normed_two + right_dot(grad_logits, w_router)
        norm_two_back = jax.vjp(rms_scale, after_attn, gain_two)[1]
        grad_after_norm, grad_gain_two = norm_two_back(grad_normed_two)
        acc_gain_two = acc_gain_two + grad_gain_two
        grad_after = upstream + grad_after_norm
        grad_branch = grad_after.astype(jnp.bfloat16)
        attended_list.append(attended)
        branch_list.append(grad_branch)
        grad_attended = (
            right_dot(grad_branch, w_out)
            .astype(jnp.bfloat16)
            .reshape(length, head_count, head_size)
        )
        scores = score_block(query_rows, key_rows, rel_bias, same_doc, score_scale)
        attn_probs = jnp.exp(scores - log_total)
        probs_low = attn_probs.astype(jnp.bfloat16)
        grad_value = jnp.einsum(
            "hqk,qhd->khd", probs_low, grad_attended, preferred_element_type=jnp.float32
        )
        grad_probs = jnp.einsum(
            "qhd,khd->hqk", grad_attended, value_rows, preferred_element_type=jnp.float32
        )
        grad_scores = attn_probs * (
            grad_probs - jnp.sum(attn_probs * grad_probs, axis=-1, keepdims=True)
        )
        flat_scores = grad_scores.reshape(head_count, length * length)
        acc_table = acc_table + jnp.dot(flat_scores, flat_hot, precision=lax.Precision.HIGHEST).T
        scores_low = grad_scores.astype(jnp.bfloat16)
        grad_query = (
            jnp.einsum("hqk,khd->qhd", scores_low, key_rows, preferred_element_type=jnp.float32)
            * score_scale
        )
        grad_key = (
            jnp.einsum("hqk,qhd->khd", scores_low, query_rows, preferred_element_type=jnp.float32)
            * score_scale
        )
        grad_packed = (
            jnp.stack([grad_query, grad_key, grad_value], axis=1)
            .reshape(length, 3 * model_width)
            .astype(jnp.bfloat16)
        )
        normed_one_list.append(normed_one)
        packed_grad_list.append(grad_packed)
        grad_normed_one = right_dot(grad_packed, w_qkv)
        norm_one_back = jax.vjp(rms_scale, inputs, gain_one)[1]
        grad_input_norm, grad_gain_one = norm_one_back(grad_normed_one)
        acc_gain_one = acc_gain_one + grad_gain_one
        grad_parts.append(grad_after + grad_input_norm)
    acc_qkv = left_dot(
        jnp.concatenate(normed_one_list, axis=0), jnp.concatenate(packed_grad_list, axis=0)
    )
    acc_out = left_dot(jnp.concatenate(attended_list, axis=0), jnp.concatenate(branch_list, axis=0))
    acc_router = left_dot(
        jnp.concatenate(normed_two_list, axis=0), jnp.concatenate(logits_list, axis=0)
    )
    acc_up = left_dot(
        jnp.concatenate(expert_in_list, axis=0), jnp.concatenate(hidden_grad_list, axis=0)
    )
    acc_down = left_dot(
        jnp.concatenate(act_list, axis=0), jnp.concatenate(expert_grad_list, axis=0)
    )
    shares = (
        lax.psum_scatter(acc_qkv, ("dp", "expert"), scatter_dimension=0, tiled=True),
        lax.psum_scatter(acc_out, ("dp", "expert"), scatter_dimension=0, tiled=True),
        lax.psum_scatter(acc_router, ("dp", "expert"), scatter_dimension=0, tiled=True),
        lax.psum_scatter(acc_gain_one, ("dp", "expert"), scatter_dimension=0, tiled=True),
        lax.psum_scatter(acc_gain_two, ("dp", "expert"), scatter_dimension=0, tiled=True),
    )
    table_total = lax.psum(acc_table, ("dp", "expert"))
    grad_up_out, grad_down_out = (acc_up[None], acc_down[None])
    return (
        jnp.concatenate(mixed_parts, axis=0),
        jnp.concatenate(grad_parts, axis=0),
        shares[0],
        shares[1],
        shares[2],
        shares[3],
        shares[4],
        table_total,
        grad_up_out,
        grad_down_out,
    )


def solution(mesh):
    in_specs = (
        P(("dp", "expert"), None),
        P(("dp", "expert"), None),
        P(("dp", "expert"), None),
        P(("dp", "expert"), None),
        P(("dp", "expert"), None),
        P(("dp", "expert"), None),
        P(("dp", "expert")),
        P(("dp", "expert")),
        P(),
        P("expert", None, "dp"),
        P("expert", "dp", None),
        P(("dp", "expert"), None),
    )
    out_specs = (
        P(("dp", "expert"), None),
        P(("dp", "expert"), None),
        P(("dp", "expert"), None),
        P(("dp", "expert"), None),
        P(("dp", "expert"), None),
        P(("dp", "expert")),
        P(("dp", "expert")),
        P(),
        P("expert", None, "dp"),
        P("expert", "dp", None),
    )
    return jax.shard_map(shards, mesh=mesh, in_specs=in_specs, out_specs=out_specs, check_vma=False)
```

profile of v0, /device:TPU:0, one launch (start us, length us, event | category | flops | bytes accessed | tf_op | source)
XLA Modules:
  0.0 636.7 jit_solution(2773071931749892204)
XLA Ops:
  16.8 42.2 %all-reduce.6 = (bf16[768]{0:T(1024)(128)(2,1)S(1)}, bf16[768]{0:T(1024)(128)(2,1)S(1)}) all-reduce(bf16[768]{0:T(1024)(128)(2,1)S(1)} %dynamic-update-slice, bf16[768]{0:T(1024)(128)(2,1)S(1)} %dynamic-update-slice.1), channel_id=1, replica_groups=mesh['dp'=4,'expert'=8] {'dp','expert'}, use_global_device_ids=true, to_apply=%add | all-reduce | flops 1536 | bytes 6144
  60.6 13.3 %all-gather.4.cloned.1.call-done = bf16[768,2304]{1,0:T(8,128)(2,1)} async-done(((bf16[24,2304]{1,0:T(8,128)(2,1)}), bf16[768,2304]{1,0:T(8,128)(2,1)}) %all-gather.4.cloned.1.call-update) | async-done | bytes 3538960 | tf_op jit(solution)/shard_map/all_gather | solution.py:50
  87.5 42.4 %all-gather.6.cloned.1.call-done = bf16[768,768]{1,0:T(8,128)(2,1)} async-done(((bf16[24,768]{1,0:T(8,128)(2,1)}), bf16[768,768]{1,0:T(8,128)(2,1)}) %all-gather.6.cloned.1.call-update) | async-done | bytes 1179664 | tf_op jit(solution)/shard_map/all_gather | solution.py:51
  137.4 15.3 %all_to_all.40 = bf16[8,20,768]{2,1,0:T(8,128)(2,1)} all-to-all(bf16[8,20,768]{2,1,0:T(8,128)(2,1)} %reshape.292), channel_id=1, replica_groups=mesh['dp'=4,'expert'=8] {'expert'}, dimensions={0} | all-to-all | bytes 491520 | tf_op jit(solution)/shard_map/all_to_all | solution.py:147
  154.3 9.6 %all_gather.33 = bf16[640,768]{1,0:T(8,128)(2,1)S(1)} all-gather(bf16[160,768]{1,0:T(8,128)(2,1)} %reshape.293), channel_id=1, replica_groups=mesh['dp'=4,'expert'=8] {'dp'}, dimensions={0}, use_global_device_ids=true | all-gather | bytes 1228800 | tf_op jit(solution)/shard_map/all_gather | solution.py:155
  172.8 4.1 all-to-all-start
  176.9 68.3 %all-gather = bf16[32,24,8]{1,2,0:T(8,128)(2,1)S(1)} all-gather(bf16[1,24,8]{1,2,0:T(8,128)(2,1)S(1)} %bitcast.212), channel_id=1, replica_groups=mesh['dp'=4,'expert'=8] {'dp','expert'}, dimensions={0}, use_global_device_ids=true | all-gather | bytes 12672 | tf_op jit(solution)/shard_map/all_gather | solution.py:52
  250.9 9.8 %all_gather.32 = bf16[640,768]{1,0:T(8,128)(2,1)S(1)} all-gather(bf16[160,768]{1,0:T(8,128)(2,1)} %reshape.287), channel_id=1, replica_groups=mesh['dp'=4,'expert'=8] {'dp'}, dimensions={0}, use_global_device_ids=true | all-gather | bytes 1228800 | tf_op jit(solution)/shard_map/all_gather | solution.py:155
  271.0 4.1 all-to-all-start.4
  277.4 8.0 %all-to-all-done.4 = bf16[8,20,768]{2,1,0:T(8,128)(2,1)} async-done(((bf16[8,20,768]{2,1,0:T(8,128)(2,1)}), bf16[8,20,768]{2,1,0:T(8,128)(2,1)}, u32[]{:S(2)}, u32[]{:S(2)}) %all-to-all-start.4) | async-done | bytes 245792 | tf_op jit(solution)/shard_map/all_to_all | solution.py:179
  287.2 9.1 %all_gather.34 = bf16[640,768]{1,0:T(8,128)(2,1)S(1)} all-gather(bf16[160,768]{1,0:T(8,128)(2,1)} %reshape.297), channel_id=1, replica_groups=mesh['dp'=4,'expert'=8] {'dp'}, dimensions={0}, use_global_device_ids=true | all-gather | bytes 1228800 | tf_op jit(solution)/shard_map/all_gather | solution.py:187
  296.3 4.1 fusion.6
  308.2 15.2 %all_to_all.41 = bf16[8,20,768]{2,1,0:T(8,128)(2,1)} all-to-all(bf16[8,20,768]{2,1,0:T(8,128)(2,1)} %reshape.301), channel_id=1, replica_groups=mesh['dp'=4,'expert'=8] {'expert'}, dimensions={0} | all-to-all | bytes 491520 | tf_op jit(solution)/shard_map/all_to_all | solution.py:179
  325.1 9.6 %all_gather.35 = bf16[640,768]{1,0:T(8,128)(2,1)S(1)} all-gather(bf16[160,768]{1,0:T(8,128)(2,1)} %reshape.302), channel_id=1, replica_groups=mesh['dp'=4,'expert'=8] {'dp'}, dimensions={0}, use_global_device_ids=true | all-gather | bytes 1228800 | tf_op jit(solution)/shard_map/all_gather | solution.py:187
  334.7 4.1 fusion.13
  348.7 8.5 %all-to-all-done.3 = bf16[8,20,768]{2,1,0:T(8,128)(2,1)S(1)} async-done(((bf16[8,20,768]{2,1,0:T(8,128)(2,1)}), bf16[8,20,768]{2,1,0:T(8,128)(2,1)S(1)}, u32[]{:S(2)}, u32[]{:S(2)}) %all-to-all-start.3) | async-done | bytes 245792 | tf_op jit(solution)/shard_map/all_to_all | solution.py:165
  357.2 4.1 all-to-all-start.1
  379.2 4.4 all-to-all-done.7
  383.7 4.1 all-to-all-start.5
  390.0 6.6 %all-to-all-done.5 = bf16[8,20,768]{2,1,0:T(8,128)(2,1)} async-done(((bf16[8,20,768]{2,1,0:T(8,128)(2,1)}), bf16[8,20,768]{2,1,0:T(8,128)(2,1)}, u32[]{:S(2)}, u32[]{:S(2)}) %all-to-all-start.5) | async-done | bytes 245792 | tf_op jit(solution)/shard_map/all_to_all | solution.py:203
  424.5 5.4 fusion.28
  447.1 40.1 %all-reduce.5 = (f32[768,8]{0,1:T(8,128)S(1)}, f32[768]{0:T(1024)S(1)}, f32[768]{0:T(1024)S(1)}, f32[32,12]{0,1:T(8,128)}) all-reduce(f32[768,8]{0,1:T(8,128)S(1)} %fusion.107, f32[768]{0:T(1024)S(1)} %add.188, f32[768]{0:T(1024)S(1)} %copy-done.68, f32[32,12]{0,1:T(8,128)S(1)} %fusion.72), channel_id=8, replica_groups=mesh['dp'=4,'expert'=8] {'dp','expert'}, use_global_device_ids=true, to_apply=%region_32.33.clone | all-reduce | flops 8064 | bytes 64512
  491.5 12.6 %reduce-scatter.18.cloned.1.call-done = f32[24,768]{1,0:T(8,128)} async-done(((f32[768,768]{1,0:T(8,128)}), f32[24,768]{1,0:T(8,128)}) %reduce-scatter.18.cloned.1.call-update) | async-done | bytes 73744 | tf_op jit(solution)/shard_map/reduce_scatter | solution.py:273
  504.1 125.3 %reduce-scatter.16.cloned.1.call-done = f32[24,2304]{1,0:T(8,128)} async-done(((f32[768,2304]{1,0:T(8,128)}), f32[24,2304]{1,0:T(8,128)}) %reduce-scatter.16.cloned.1.call-update) | async-done | bytes 221200 | tf_op jit(solution)/shard_map/reduce_scatter | solution.py:272
  (411 shorter events, 150.3 us)
Async XLA Ops:
  7.2 156.8 %copy-start = (bf16[1,768,768]{2,1,0:T(8,128)(2,1)S(1)}, bf16[1,768,768]{2,1,0:T(8,128)(2,1)}, u32[]{:S(2)}) copy-start(bf16[1,768,768]{2,1,0:T(8,128)(2,1)} %param.22) | copy-start | bytes 3538948
  7.2 66.8 %all-gather.4.cloned.1.call-start = ((), (), s32[]{:S(2)}) async-start(), calls=%async_computation.14 | async-start | bytes 3649536 | tf_op jit(solution)/shard_map/all_gather | solution.py:50
  7.9 121.9 %all-gather.6.cloned.1.call-start = ((), (), s32[]{:S(2)}) async-start(), calls=%async_computation.15 | async-start | bytes 1216512 | tf_op jit(solution)/shard_map/all_gather | solution.py:51
  8.7 333.1 %reduce-scatter.10.cloned.1.call-start = ((), (), s32[]{:S(2)}) async-start(), calls=%async_computation.17 | async-start | bytes 1228800 | tf_op jit(solution)/shard_map/reduce_scatter | solution.py:158
  11.4 49.0 %copy-start.98 = (f32[128]{0:T(128)}, f32[128]{0:T(128)S(1)}, u32[]{:S(2)}) copy-start(f32[128]{0:T(128)S(1)} %fusion.144) | copy-start | bytes 1540
  15.3 45.1 %copy-start.6 = (bf16[256,768]{1,0:T(8,128)(2,1)S(1)}, bf16[256,768]{1,0:T(8,128)(2,1)}, u32[]{:S(2)}) copy-start(bf16[256,768]{1,0:T(8,128)(2,1)} %param.13) | copy-start | bytes 1179652
  16.2 117.8 %copy-start.69 = (s32[128]{0:T(128)}, s32[128]{0:T(128)S(1)}, u32[]{:S(2)}) copy-start(s32[128]{0:T(128)S(1)} %get-tuple-element.42) | copy-start | bytes 1540
  16.2 153.0 %copy-start.75 = (s32[128]{0:T(128)}, s32[128]{0:T(128)S(1)}, u32[]{:S(2)}) copy-start(s32[128]{0:T(128)S(1)} %get-tuple-element.41) | copy-start | bytes 1540
  16.3 57.7 %copy-start.101 = (f32[128]{0:T(128)}, f32[128]{0:T(128)S(1)}, u32[]{:S(2)}) copy-start(f32[128]{0:T(128)S(1)} %fusion.146) | copy-start | bytes 1540
  172.8 76.4 %all-to-all-start = ((bf16[8,20,768]{2,1,0:T(8,128)(2,1)}), bf16[8,20,768]{2,1,0:T(8,128)(2,1)}, u32[]{:S(2)}, u32[]{:S(2)}) async-start(bf16[8,20,768]{2,1,0:T(8,128)(2,1)} %reshape.286), calls=%async_computation | async-start | bytes 589824 | tf_op jit(solution)/shard_map/all_to_all | solution.py:147
  176.9 170.1 %reduce-scatter.8.cloned.1.call-start = ((), (), s32[]{:S(2)}) async-start(), calls=%async_computation.16 | async-start | bytes 1228800 | tf_op jit(solution)/shard_map/reduce_scatter | solution.py:158
  271.0 14.4 %all-to-all-start.4 = ((bf16[8,20,768]{2,1,0:T(8,128)(2,1)}), bf16[8,20,768]{2,1,0:T(8,128)(2,1)}, u32[]{:S(2)}, u32[]{:S(2)}) async-start(bf16[8,20,768]{2,1,0:T(8,128)(2,1)} %reshape.296), calls=%async_computation.6 | async-start | bytes 589824 | tf_op jit(solution)/shard_map/all_to_all | solution.py:179
  275.1 86.8 %reduce-scatter.12.cloned.1.call-start = ((), (), s32[]{:S(2)}) async-start(), calls=%async_computation.18 | async-start | bytes 1228800 | tf_op jit(solution)/shard_map/reduce_scatter | solution.py:194
  303.3 60.9 %reduce-scatter.14.cloned.1.call-start = ((), (), s32[]{:S(2)}) async-start(), calls=%async_computation.19 | async-start | bytes 1228800 | tf_op jit(solution)/shard_map/reduce_scatter | solution.py:194
  343.5 13.7 %all-to-all-start.3 = ((bf16[8,20,768]{2,1,0:T(8,128)(2,1)}), bf16[8,20,768]{2,1,0:T(8,128)(2,1)S(1)}, u32[]{:S(2)}, u32[]{:S(2)}) async-start(bf16[8,20,768]{2,1,0:T(8,128)(2,1)} %reshape.294), calls=%async_computation.5 | async-start | bytes 589824 | tf_op jit(solution)/shard_map/all_to_all | solution.py:165
  357.2 13.7 %all-to-all-start.1 = ((bf16[8,20,768]{2,1,0:T(8,128)(2,1)}), bf16[8,20,768]{2,1,0:T(8,128)(2,1)}, u32[]{:S(2)}, u32[]{:S(2)}) async-start(bf16[8,20,768]{2,1,0:T(8,128)(2,1)} %reshape.288), calls=%async_computation.2 | async-start | bytes 589824 | tf_op jit(solution)/shard_map/all_to_all | solution.py:165
  370.9 12.8 %all-to-all-start.7 = ((bf16[8,20,768]{2,1,0:T(8,128)(2,1)}), bf16[8,20,768]{2,1,0:T(8,128)(2,1)S(1)}, u32[]{:S(2)}, u32[]{:S(2)}) async-start(bf16[8,20,768]{2,1,0:T(8,128)(2,1)} %reshape.303), calls=%async_computation.11 | async-start | bytes 589824 | tf_op jit(solution)/shard_map/all_to_all | solution.py:203
  383.7 13.0 %all-to-all-start.5 = ((bf16[8,20,768]{2,1,0:T(8,128)(2,1)}), bf16[8,20,768]{2,1,0:T(8,128)(2,1)}, u32[]{:S(2)}, u32[]{:S(2)}) async-start(bf16[8,20,768]{2,1,0:T(8,128)(2,1)} %reshape.298), calls=%async_computation.8 | async-start | bytes 589824 | tf_op jit(solution)/shard_map/all_to_all | solution.py:203
  387.7 116.4 %reduce-scatter.18.cloned.1.call-start = ((), (), s32[]{:S(2)}) async-start(), calls=%async_computation.21 | async-start | bytes 2433024 | tf_op jit(solution)/shard_map/reduce_scatter | solution.py:273
  406.3 223.1 %reduce-scatter.16.cloned.1.call-start = ((), (), s32[]{:S(2)}) async-start(), calls=%async_computation.20 | async-start | bytes 7299072 | tf_op jit(solution)/shard_map/reduce_scatter | solution.py:272
  445.2 43.9 %copy-start.106 = (f32[128]{0:T(128)S(1)}, f32[128]{0:T(128)}, u32[]{:S(2)}) copy-start(f32[128]{0:T(128)} %copy-done.105) | copy-start | bytes 1540
  445.2 43.9 %copy-start.108 = (f32[128]{0:T(128)S(1)}, f32[128]{0:T(128)}, u32[]{:S(2)}) copy-start(f32[128]{0:T(128)} %copy-done.107) | copy-start | bytes 1540
  445.2 43.9 %copy-start.16 = (bf16[256,768]{1,0:T(8,128)(2,1)S(1)}, bf16[256,768]{1,0:T(8,128)(2,1)}, u32[]{:S(2)}) copy-start(bf16[256,768]{1,0:T(8,128)(2,1)} %param.24) | copy-start | bytes 1179652
  489.5 139.9 %copy-start.1 = (bf16[1,768,768]{2,1,0:T(8,128)(2,1)S(1)}, bf16[1,768,768]{2,1,0:T(8,128)(2,1)}, u32[]{:S(2)}) copy-start(bf16[1,768,768]{2,1,0:T(8,128)(2,1)} %param.22) | copy-start | bytes 3538948
  (118 other events, 1105.9 us)
Sparse Core Ops, SparseCore 0:
  10.9 62.9 all-gather.3
  76.9 52.9 all-gather.5
  169.4 22.3 reduce-scatter.9
  266.1 21.1 reduce-scatter.7
  303.4 23.3 reduce-scatter.11
  341.9 22.3 reduce-scatter.13
  406.4 97.6 reduce-scatter.17
  511.3 118.0 reduce-scatter.15
where the time goes:
time: 646 us; the launch traced here: 637 us
  waiting for transfers between devices  226 us (35%)
  blocking collectives  219 us (34%)
  matrix products  83.6 us (13%)
  local copies, waits for them, and re-layouts  52.7 us (8%)
  starting transfers between devices  23.8 us (4%)
  between operations  16.2 us (3%)
  other arithmetic  14.9 us (2%)
    reduce_scatter x1, waiting for transfers between devices, shards(): lax.psum_scatter(acc_qkv, ('dp', 'expert'), scatter_dimension=0, tiled=True)  125 us
    unnamed x2, blocking collectives  82.3 us
    all_gather x1, blocking collectives, gather_dense(): lax.all_gather(router_weight, ('dp', 'expert'), axis=0, tiled=True)  68.3 us
    all_gather x1, waiting for transfers between devices, gather_dense(): lax.all_gather(out_weight, ('dp', 'expert'), axis=0, tiled=True)  42.4 us
    dot_general x10, matrix products, right_dot(): lax.dot_general(left, right, (((1,), (1,)), ((), ())), preferred_element_...  21.5 us
    dot_general x9, matrix products, left_dot(): lax.dot_general(left, right, (((0,), (0,)), ((), ())), preferred_element_...  21.3 us
    all_gather x2, blocking collectives, shards(): expert_in = lax.all_gather(received, 'dp', axis=0, tiled=True)  19.4 us
    all_gather x2, blocking collectives, shards(): grad_expert_out = lax.all_gather(grad_back, 'dp', axis=0, tiled=True)  18.8 us
  transfers between devices with their start and end apart: 14, of which 10 were waited for; matrix products, arithmetic and copies ran while one was open for 19% of the time, Pallas kernels for 0%

commit v1 on v0

v1 whole, which is shorter than its diff:
```python
import jax
import jax.numpy as jnp
import numpy as np
from jax import lax
from jax.sharding import PartitionSpec as P

EPS = 1e-06
MASKED = -1e30


def bucket_onehot(length, buckets):
    half_count = buckets // 2
    exact_count = half_count // 2
    offsets = np.arange(length)[None, :] - np.arange(length)[:, None]
    distance = np.abs(offsets)
    scaled = (
        np.log(np.maximum(distance, 1) / exact_count)
        / np.log(128.0 / exact_count)
        * (half_count - exact_count)
    )
    far_bucket = np.minimum(exact_count + np.floor(scaled).astype(np.int32), half_count - 1)
    bucket = np.where(distance < exact_count, distance, far_bucket) + np.where(
        offsets > 0, half_count, 0
    )
    return (bucket[:, :, None] == np.arange(buckets)[None, None, :]).astype(np.float32)


def rms_scale(values, gain_vec):
    return values * lax.rsqrt(jnp.mean(values * values, axis=-1, keepdims=True) + EPS) * gain_vec


def gelu_tanh(values):
    return jax.nn.gelu(values, approximate=True)


def left_dot(left, right):
    return lax.dot_general(
        left, right, (((0,), (0,)), ((), ())), preferred_element_type=jnp.float32
    )


def right_dot(left, right):
    return lax.dot_general(
        left, right, (((1,), (1,)), ((), ())), preferred_element_type=jnp.float32
    )


def shards(
    tokens,
    segments,
    routes,
    qkv_weight,
    out_weight,
    router_weight,
    attn_gain,
    moe_gain,
    bias_table,
    up_weight,
    down_weight,
    cotangent,
):
    both = ("dp", "expert")
    micro_count, length = segments.shape
    rows, model_width = tokens.shape
    buckets, head_count = bias_table.shape
    head_size = model_width // head_count
    score_scale = head_size ** (-0.5)
    experts = router_weight.shape[1]
    capacity = max(2, (5 * length + 4 * experts - 1) // (4 * experts))
    packed_width = qkv_weight.shape[1]
    side_pad = (-(experts + 2)) % 128

    first_part = jnp.concatenate(
        [
            qkv_weight,
            router_weight,
            attn_gain[:, None],
            moe_gain[:, None],
            jnp.zeros((qkv_weight.shape[0], side_pad), jnp.bfloat16),
        ],
        axis=1,
    )
    first_whole = lax.all_gather(first_part, both, axis=0, tiled=True)
    w_out = lax.all_gather(out_weight, both, axis=0, tiled=True)
    w_qkv = first_whole[:, :packed_width]
    side = first_whole[:, packed_width:]
    w_router = side[:, :experts]
    gain_one = side[:, experts].astype(jnp.float32)
    gain_two = side[:, experts + 1].astype(jnp.float32)
    up_mat, down_mat = (up_weight[0], down_weight[0])

    bucket_hot = bucket_onehot(length, buckets)
    flat_hot = jnp.asarray(bucket_hot.reshape(length * length, buckets).astype(jnp.bfloat16))
    rel_bias = jnp.dot(flat_hot, bias_table, preferred_element_type=jnp.float32)
    rel_bias = rel_bias.reshape(length, length, head_count).transpose(2, 0, 1)

    inputs = tokens.astype(jnp.float32)
    upstream = cotangent.astype(jnp.float32)
    same_doc = segments[:, :, None] == segments[:, None, :]
    route_ids = routes[:, 0]
    route_hot = (route_ids[:, None] == jnp.arange(experts, dtype=jnp.int32)[None, :]).astype(
        jnp.float32
    )
    earlier = (
        (np.arange(rows)[:, None] > np.arange(rows)[None, :])
        & (np.arange(rows)[:, None] // length == np.arange(rows)[None, :] // length)
    ).astype(np.float32)
    same_route = route_ids[:, None] == route_ids[None, :]
    slot_index = jnp.sum(jnp.where(same_route, jnp.asarray(earlier), 0.0), axis=1).astype(jnp.int32)
    slab_index = jnp.arange(rows, dtype=jnp.int32) // length
    position = (route_ids * micro_count + slab_index) * capacity + slot_index
    slots = experts * micro_count * capacity
    dispatch = (jnp.arange(slots, dtype=jnp.int32)[:, None] == position[None, :]).astype(
        jnp.bfloat16
    )

    normed_one = rms_scale(inputs, gain_one).astype(jnp.bfloat16)
    packed = jnp.dot(normed_one, w_qkv, preferred_element_type=jnp.float32).astype(jnp.bfloat16)
    packed = packed.reshape(micro_count, length, 3, head_count, head_size)
    query_rows, key_rows, value_rows = (packed[:, :, 0], packed[:, :, 1], packed[:, :, 2])
    scores = (
        jnp.einsum("bqhd,bkhd->bhqk", query_rows, key_rows, preferred_element_type=jnp.float32)
        * score_scale
    )
    scores = jnp.where(same_doc[:, None], scores + rel_bias[None], MASKED)
    expo = jnp.exp(scores - jnp.max(scores, axis=-1, keepdims=True))
    attn_probs = expo / jnp.sum(expo, axis=-1, keepdims=True)
    probs_low = attn_probs.astype(jnp.bfloat16)
    attended = (
        jnp.einsum("bhqk,bkhd->bqhd", probs_low, value_rows, preferred_element_type=jnp.float32)
        .astype(jnp.bfloat16)
        .reshape(rows, model_width)
    )
    after_attn = inputs + jnp.dot(attended, w_out, preferred_element_type=jnp.float32)
    normed_two = rms_scale(after_attn, gain_two).astype(jnp.bfloat16)
    logits = jnp.dot(normed_two, w_router, preferred_element_type=jnp.float32)
    router_probs = jax.nn.softmax(logits, axis=-1)
    gate_prob = jnp.sum(router_probs * route_hot, axis=1, keepdims=True)
    grad_token_out = (gate_prob * upstream).astype(jnp.bfloat16)

    sent = jnp.dot(
        dispatch,
        jnp.concatenate([normed_two, grad_token_out], axis=1),
        preferred_element_type=jnp.float32,
    ).astype(jnp.bfloat16)
    received = lax.all_to_all(
        sent.reshape(experts, micro_count * capacity, 2 * model_width),
        "expert",
        split_axis=0,
        concat_axis=0,
        tiled=True,
    ).reshape(slots, 2 * model_width)
    expert_rows = lax.all_gather(received, "dp", axis=0, tiled=True)
    expert_in, grad_expert_out = (expert_rows[:, :model_width], expert_rows[:, model_width:])
    hidden = jnp.dot(expert_in, up_mat, preferred_element_type=jnp.float32)
    act, act_back = jax.vjp(gelu_tanh, hidden)
    act_low = act.astype(jnp.bfloat16)
    grad_activation = right_dot(grad_expert_out, down_mat)
    grad_hidden = act_back(grad_activation)[0].astype(jnp.bfloat16)
    results = jnp.concatenate(
        [
            jnp.dot(act_low, down_mat, preferred_element_type=jnp.float32).astype(jnp.bfloat16),
            right_dot(grad_hidden, up_mat).astype(jnp.bfloat16),
        ],
        axis=1,
    )
    results = lax.psum_scatter(results, "dp", scatter_dimension=0, tiled=True)
    returned = lax.all_to_all(
        results.reshape(experts, micro_count * capacity, 2 * model_width),
        "expert",
        split_axis=0,
        concat_axis=0,
        tiled=True,
    ).reshape(slots, 2 * model_width)
    acc_up = left_dot(expert_in, grad_hidden)
    acc_down = left_dot(act_low, grad_expert_out)
    back = left_dot(dispatch, returned)
    combined, grad_normed_two = (back[:, :model_width], back[:, model_width:])
    mixed = (after_attn + gate_prob * combined).astype(jnp.bfloat16)
    grad_gate = jnp.sum(upstream * combined, axis=1, keepdims=True)
    grad_logits = (router_probs * (route_hot - gate_prob) * grad_gate).astype(jnp.bfloat16)
    grad_normed_two = grad_normed_two + right_dot(grad_logits, w_router)
    grad_after_norm, grad_gain_two = jax.vjp(rms_scale, after_attn, gain_two)[1](grad_normed_two)
    grad_after = upstream + grad_after_norm
    grad_branch = grad_after.astype(jnp.bfloat16)

    acc_out = left_dot(attended, grad_branch)
    acc_router = left_dot(normed_two, grad_logits)
    out_share = lax.psum_scatter(
        jnp.concatenate(
            [
                acc_out,
                acc_router,
                grad_gain_two[:, None],
                jnp.zeros((model_width, (-(experts + 1)) % 128), jnp.float32),
            ],
            axis=1,
        ).astype(jnp.bfloat16),
        both,
        scatter_dimension=0,
        tiled=True,
    ).astype(jnp.float32)

    grad_attended = (
        right_dot(grad_branch, w_out)
        .astype(jnp.bfloat16)
        .reshape(micro_count, length, head_count, head_size)
    )
    grad_value = jnp.einsum(
        "bhqk,bqhd->bkhd", probs_low, grad_attended, preferred_element_type=jnp.float32
    )
    grad_probs = jnp.einsum(
        "bqhd,bkhd->bhqk", grad_attended, value_rows, preferred_element_type=jnp.float32
    )
    grad_scores = attn_probs * (
        grad_probs - jnp.sum(attn_probs * grad_probs, axis=-1, keepdims=True)
    )
    scores_low = grad_scores.astype(jnp.bfloat16)
    grad_query = (
        jnp.einsum("bhqk,bkhd->bqhd", scores_low, key_rows, preferred_element_type=jnp.float32)
        * score_scale
    )
    grad_key = (
        jnp.einsum("bhqk,bqhd->bkhd", scores_low, query_rows, preferred_element_type=jnp.float32)
        * score_scale
    )
    grad_packed = (
        jnp.stack([grad_query, grad_key, grad_value], axis=2)
        .reshape(rows, packed_width)
        .astype(jnp.bfloat16)
    )
    grad_normed_one = right_dot(grad_packed, w_qkv)
    grad_input_norm, grad_gain_one = jax.vjp(rms_scale, inputs, gain_one)[1](grad_normed_one)
    grad_tokens = grad_after + grad_input_norm
    acc_qkv = left_dot(normed_one, grad_packed)
    qkv_share = lax.psum_scatter(
        jnp.concatenate(
            [
                acc_qkv.astype(jnp.bfloat16),
                grad_gain_one[:, None].astype(jnp.bfloat16),
                jnp.zeros((model_width, 127), jnp.bfloat16),
            ],
            axis=1,
        ),
        both,
        scatter_dimension=0,
        tiled=True,
    ).astype(jnp.float32)

    flat_scores = jnp.sum(grad_scores, axis=0).reshape(head_count, length * length)
    high = flat_scores.astype(jnp.bfloat16)
    low = (flat_scores - high.astype(jnp.float32)).astype(jnp.bfloat16)
    table_parts = jnp.dot(
        jnp.concatenate([high, low], axis=0), flat_hot, preferred_element_type=jnp.float32
    )
    acc_table = (table_parts[:head_count] + table_parts[head_count:]).T
    table_total = lax.psum(acc_table, both)
    return (
        mixed,
        grad_tokens,
        qkv_share[:, :packed_width],
        out_share[:, :model_width],
        out_share[:, model_width : model_width + experts],
        qkv_share[:, packed_width],
        out_share[:, model_width + experts],
        table_total,
        acc_up[None],
        acc_down[None],
    )


def solution(mesh):
    in_specs = (
        P(("dp", "expert"), None),
        P(("dp", "expert"), None),
        P(("dp", "expert"), None),
        P(("dp", "expert"), None),
        P(("dp", "expert"), None),
        P(("dp", "expert"), None),
        P(("dp", "expert")),
        P(("dp", "expert")),
        P(),
        P("expert", None, "dp"),
        P("expert", "dp", None),
        P(("dp", "expert"), None),
    )
    out_specs = (
        P(("dp", "expert"), None),
        P(("dp", "expert"), None),
        P(("dp", "expert"), None),
        P(("dp", "expert"), None),
        P(("dp", "expert"), None),
        P(("dp", "expert")),
        P(("dp", "expert")),
        P(),
        P("expert", None, "dp"),
        P("expert", "dp", None),
    )
    return jax.shard_map(shards, mesh=mesh, in_specs=in_specs, out_specs=out_specs, check_vma=False)
```

time: 646 us -> 551 us (0.85); the launches traced: 637 us -> 550 us
  blocking collectives: 219 us -> 66.8 us
  waiting for transfers between devices: 226 us -> 360 us
  matrix products: 83.6 us -> 49.7 us
  starting transfers between devices: 23.8 us -> 6.42 us
  local copies, waits for them, and re-layouts: 52.7 us -> 36.4 us
    unnamed x8, waiting for transfers between devices: 1.48 us -> 171 us
    all_gather x5 -> x0, blocking collectives: 106 us -> none  [the longest x1 68.3 us: gather_dense(): lax.all_gather(router_weight, ('dp', 'expert'), axis=0, tiled=True)]
    reduce_scatter x6 -> x1, waiting for transfers between devices: 139 us -> 43 us  [shards(): results = lax.psum_scatter(results, 'dp', scatter_dimension=0, tiled=True)]
    unnamed x2 -> x0, blocking collectives: 82.3 us -> none
    all_gather x2 -> x3, waiting for transfers between devices: 55.7 us -> 129 us  [the longest x1 57.2 us: shards(): first_whole = lax.all_gather(first_part, both, axis=0, tiled=True)]
    psum x0 -> x1, blocking collectives: none -> 37.7 us  [shards(): table_total = lax.psum(acc_table, both)]
    reshape x18 -> x4, local copies, waits for them, and re-layouts: 27.8 us -> 1.61 us  [the longest x2 1.2 us: shards(): rel_bias = rel_bias.reshape(length, length, head_count).transpose(2, 0, 1)]
    all_to_all x6 -> x1, starting transfers between devices: 23.3 us -> 5.52 us  [shards(): lax.all_to_all(results.reshape(experts, micro_count * capacity, 2 * model...]
  transfers between devices with their start and end apart: 14 -> 7, of which waited for: 10 -> 7; matrix products, arithmetic and copies ran while one was open for 19% -> 9% of each run, Pallas kernels for 0% -> 0%
where the time goes in v1:
time: 551 us; the launch traced here: 550 us
  waiting for transfers between devices  360 us (65%)
  blocking collectives  66.8 us (12%)
  matrix products  49.7 us (9%)
  local copies, waits for them, and re-layouts  36.4 us (7%)
  other arithmetic  16 us (3%)
  between operations  14.8 us (3%)
  starting transfers between devices  6.42 us (1%)
    unnamed x8, waiting for transfers between devices  171 us
    all_gather x1, waiting for transfers between devices, shards(): first_whole = lax.all_gather(first_part, both, axis=0, tiled=True)  57.2 us
    reduce_scatter x1, waiting for transfers between devices, shards(): results = lax.psum_scatter(results, 'dp', scatter_dimension=0, tiled=True)  43 us
    all_gather x1, waiting for transfers between devices, shards(): w_out = lax.all_gather(out_weight, both, axis=0, tiled=True)  40.7 us
    psum x1, blocking collectives, shards(): table_total = lax.psum(acc_table, both)  37.7 us
    all_gather x1, waiting for transfers between devices, shards(): expert_rows = lax.all_gather(received, 'dp', axis=0, tiled=True)  30.9 us
    all_to_all x1, blocking collectives, shards(): lax.all_to_all(sent.reshape(experts, micro_count * capacity, 2 * model_wi...  29.1 us
    dot_general x6, matrix products, left_dot(): lax.dot_general(left, right, (((0,), (0,)), ((), ())), preferred_element_...  17.7 us
  transfers between devices with their start and end apart: 7, of which 7 were waited for; matrix products, arithmetic and copies ran while one was open for 9% of the time, Pallas kernels for 0%

profile of v1, /device:TPU:0, one launch (start us, length us, event | category | flops | bytes accessed | tf_op | source)
XLA Modules:
  0.0 550.0 jit_solution(14939796613339292089)
XLA Ops:
  17.7 57.2 %all-gather.4.cloned.1.call-done = bf16[768,2432]{1,0:T(8,128)(2,1)} async-done(((bf16[24,2432]{1,0:T(8,128)(2,1)}), bf16[768,2432]{1,0:T(8,128)(2,1)}) %all-gather.4.cloned.1.call-update) | async-done | bytes 3735568 | tf_op jit(solution)/shard_map/all_gather | solution.py:83
  77.4 4.1 convolution_convert_fusion.1
  88.1 2.1 copy.108
  90.3 40.7 %all-gather.6.cloned.1.call-done = bf16[768,768]{1,0:T(8,128)(2,1)} async-done(((bf16[24,768]{1,0:T(8,128)(2,1)}), bf16[768,768]{1,0:T(8,128)(2,1)}) %all-gather.6.cloned.1.call-update) | async-done | bytes 1179664 | tf_op jit(solution)/shard_map/all_gather | solution.py:84
  130.9 2.0 multiply_reduce_fusion.3
  135.0 29.1 %all_to_all.10 = bf16[8,40,1536]{2,1,0:T(8,128)(2,1)} all-to-all(bf16[8,40,1536]{2,1,0:T(8,128)(2,1)S(1)} %bitcast.119), channel_id=1, replica_groups=mesh['dp'=4,'expert'=8] {'expert'}, dimensions={0} | all-to-all | bytes 1966080 | tf_op jit(solution)/shard_map/all_to_all | solution.py:146
  164.4 30.9 %all-gather.8.cloned.1.call-done = bf16[1280,1536]{1,0:T(8,128)(2,1)} async-done(((bf16[320,1536]{1,0:T(8,128)(2,1)}), bf16[1280,1536]{1,0:T(8,128)(2,1)}) %all-gather.8.cloned.1.call-update) | async-done | bytes 3932176 | tf_op jit(solution)/shard_map/all_gather | solution.py:153
  195.3 3.6 fusion.19
  202.5 3.7 fusion.7
  209.2 2.2 pad_maximum_fusion
  211.4 6.2 %copy.124 = bf16[1280,1536]{1,0:T(8,128)(2,1)} copy(bf16[1280,1536]{0,1:T(8,128)(2,1)} %pad_maximum_fusion) | data formatting | bytes 7864320
  217.6 43.0 %reduce-scatter.8.cloned.1.call-done = bf16[320,1536]{1,0:T(8,128)(2,1)} async-done(((bf16[1280,1536]{1,0:T(8,128)(2,1)}), bf16[320,1536]{1,0:T(8,128)(2,1)}) %reduce-scatter.8.cloned.1.call-update) | async-done | bytes 983056 | tf_op jit(solution)/shard_map/reduce_scatter | solution.py:167
  260.7 5.5 %all-to-all-start.1 = ((bf16[8,40,1536]{2,1,0:T(8,128)(2,1)}), bf16[8,40,1536]{2,1,0:T(8,128)(2,1)S(1)}, u32[]{:S(2)}, u32[]{:S(2)}) async-start(bf16[8,40,1536]{2,1,0:T(8,128)(2,1)} %bitcast.118), calls=%async_computation.1 | async-start | bytes 1966080 | tf_op jit(solution)/shard_map/all_to_all | solution.py:168
  267.1 6.2 %fusion.25 = f32[1,768,768]{2,1,0:T(8,128)} fusion(bf16[1280,1536]{1,0:T(8,128)(2,1)} %all-gather.8.cloned.1.call-done, f32[1280,768]{1,0:T(8,128)} %copy-done.45), kind=kOutput, calls=%fused_computation.30 | convolution fusion | flops 1518796800 | bytes 8257536 | tf_op jit(solution)/shard_map/dot_general | solution.py:37
  273.3 17.3 %all-to-all-done.1 = bf16[8,40,1536]{2,1,0:T(8,128)(2,1)S(1)} async-done(((bf16[8,40,1536]{2,1,0:T(8,128)(2,1)}), bf16[8,40,1536]{2,1,0:T(8,128)(2,1)S(1)}, u32[]{:S(2)}, u32[]{:S(2)}) %all-to-all-start.1) | async-done | bytes 983072 | tf_op jit(solution)/shard_map/all_to_all | solution.py:168
  292.9 2.0 multiply_reduce_fusion.1
  298.3 3.4 fusion.34
  308.7 2.1 fusion.46
  311.0 3.1 convolution_convert_fusion
  314.1 6.5 %concatenate.22 = bf16[768,2432]{1,0:T(8,128)(2,1)} concatenate(bf16[768,2304]{1,0:T(8,128)(2,1)} %convolution_convert_fusion, bf16[768,1]{1,0:T(8,128)(2,1)S(1)} %convert_element_type.161, bf16[768,127]{1,0:T(8,128)(2,1)S(1)} %broadcast_in_dim.78), dimensions={1} | concatenate | bytes 7471104 | tf_op jit(solution)/shard_map/concatenate | solution.py:237
  320.7 5.4 fusion.22
  328.2 37.7 %psum.7 = f32[32,12]{0,1:T(8,128)} all-reduce(f32[32,12]{0,1:T(8,128)S(1)} %fusion.77), channel_id=1, replica_groups=mesh['dp'=4,'expert'=8] {'dp','expert'}, use_global_device_ids=true, to_apply=%region_18.19 | all-reduce | flops 384 | bytes 3072 | tf_op jit(solution)/shard_map/psum | solution.py:257
  367.0 68.6 %all-reduce.4.cloned.1.call-done = bf16[768,896]{0,1:T(8,128)(2,1)} async-done(((bf16[768,896]{0,1:T(8,128)(2,1)}), bf16[768,896]{0,1:T(8,128)(2,1)}) %all-reduce.4.cloned.1.call-update) | async-done | bytes 1376272
  438.7 101.3 %reduce-scatter.10.cloned.1.call-done = bf16[24,2432]{1,0:T(8,128)(2,1)} async-done(((bf16[768,2432]{1,0:T(8,128)(2,1)}), bf16[24,2432]{1,0:T(8,128)(2,1)}) %reduce-scatter.10.cloned.1.call-update) | async-done | bytes 116752
  (173 shorter events, 51.0 us)
Async XLA Ops:
  7.2 191.7 %copy-start = (bf16[1,768,768]{2,1,0:T(8,128)(2,1)S(1)}, bf16[1,768,768]{2,1,0:T(8,128)(2,1)}, u32[]{:S(2)}) copy-start(bf16[1,768,768]{2,1,0:T(8,128)(2,1)} %param.24) | copy-start | bytes 3538948
  7.2 67.7 %all-gather.4.cloned.1.call-start = ((), (), s32[]{:S(2)}) async-start(), calls=%async_computation.4 | async-start | bytes 3852288 | tf_op jit(solution)/shard_map/all_gather | solution.py:83
  11.2 119.7 %all-gather.6.cloned.1.call-start = ((), (), s32[]{:S(2)}) async-start(), calls=%async_computation.5 | async-start | bytes 1216512 | tf_op jit(solution)/shard_map/all_gather | solution.py:84
  12.0 183.3 %all-gather.8.cloned.1.call-start = ((), (), s32[]{:S(2)}) async-start(), calls=%async_computation.6 | async-start | bytes 4915200 | tf_op jit(solution)/shard_map/all_gather | solution.py:153
  13.2 3.2 copy-start.35
  15.0 62.5 %copy-start.5 = (bf16[256,768]{1,0:T(8,128)(2,1)S(1)}, bf16[256,768]{1,0:T(8,128)(2,1)}, u32[]{:S(2)}) copy-start(bf16[256,768]{1,0:T(8,128)(2,1)} %param.14) | copy-start | bytes 1179652
  16.4 65.2 %copy-start.33 = (f32[256]{0:T(256)}, f32[256]{0:T(256)S(1)}, u32[]{:S(2)}) copy-start(f32[256]{0:T(256)S(1)} %fusion.83) | copy-start | bytes 3076
  85.1 3.0 copy-start.2
  86.8 44.2 %copy-start.6 = (bf16[256,768]{1,0:T(8,128)(2,1)S(1)}, bf16[256,768]{1,0:T(8,128)(2,1)}, u32[]{:S(2)}) copy-start(bf16[256,768]{1,0:T(8,128)(2,1)} %param.14) | copy-start | bytes 1179652
  90.3 42.7 %copy-start.25 = (f32[768]{0:T(1024)S(1)}, f32[768]{0:T(1024)}, u32[]{:S(2)}) copy-start(f32[768]{0:T(1024)} %get-tuple-element.60) | copy-start | bytes 9220
  130.9 3.5 copy-start.31
  130.9 3.5 copy-start.12
  164.2 96.5 %reduce-scatter.8.cloned.1.call-start = ((), (), s32[]{:S(2)}) async-start(), calls=%async_computation.7 | async-start | bytes 4915200 | tf_op jit(solution)/shard_map/reduce_scatter | solution.py:167
  198.9 3.5 copy-start.43
  202.5 5.0 copy-start.44
  260.7 29.9 %all-to-all-start.1 = ((bf16[8,40,1536]{2,1,0:T(8,128)(2,1)}), bf16[8,40,1536]{2,1,0:T(8,128)(2,1)S(1)}, u32[]{:S(2)}, u32[]{:S(2)}) async-start(bf16[8,40,1536]{2,1,0:T(8,128)(2,1)} %bitcast.118), calls=%async_computation.1 | async-start | bytes 1966080 | tf_op jit(solution)/shard_map/all_to_all | solution.py:168
  266.2 169.4 %all-reduce.4.cloned.1.call-start = ((), (), s32[]{:S(2)}) async-start(), calls=%async_computation.8 | async-start | bytes 2752512
  298.3 3.5 copy-start.3
  298.3 3.4 copy-start.20
  306.3 233.7 %reduce-scatter.10.cloned.1.call-start = ((), (), s32[]{:S(2)}) async-start(), calls=%async_computation.9 | async-start | bytes 3852288
  320.7 5.4 copy-start.13
  327.1 38.7 %copy-start.36 = (f32[256]{0:T(256)S(1)}, f32[256]{0:T(256)}, u32[]{:S(2)}) copy-start(f32[256]{0:T(256)} %copy-done.35) | copy-start | bytes 3076
  327.1 38.7 %copy-start.18 = (f32[256,768]{1,0:T(8,128)S(1)}, f32[256,768]{1,0:T(8,128)}, u32[]{:S(2)}) copy-start(f32[256,768]{1,0:T(8,128)} %get-tuple-element.84) | copy-start | bytes 2359300
  365.9 177.3 %copy-start.1 = (bf16[1,768,768]{2,1,0:T(8,128)(2,1)S(1)}, bf16[1,768,768]{2,1,0:T(8,128)(2,1)}, u32[]{:S(2)}) copy-start(bf16[1,768,768]{2,1,0:T(8,128)(2,1)} %param.24) | copy-start | bytes 3538948
  (30 other events, 48.8 us)
Sparse Core Ops, SparseCore 0:
  11.5 63.4 all-gather.3
  77.8 53.0 all-gather.5
  164.3 30.9 all-gather.7
  217.7 42.8 reduce-scatter.7
  306.3 129.2 all-reduce.3
  442.1 97.8 reduce-scatter.9

commit v2 on v1

--- a/solution.py
+++ b/solution.py
@@ -43,6 +43,11 @@
     return lax.dot_general(
         left, right, (((1,), (1,)), ((), ())), preferred_element_type=jnp.float32
     )
+
+
+def two_terms(values):
+    high = lax.reduce_precision(values, exponent_bits=8, mantissa_bits=7)
+    return high.astype(jnp.bfloat16), (values - high).astype(jnp.bfloat16)
 
 
 def shards(
@@ -59,7 +64,6 @@
     down_weight,
     cotangent,
 ):
-    both = ("dp", "expert")
     micro_count, length = segments.shape
     rows, model_width = tokens.shape
     buckets, head_count = bias_table.shape
@@ -80,8 +84,12 @@
         ],
         axis=1,
     )
-    first_whole = lax.all_gather(first_part, both, axis=0, tiled=True)
-    w_out = lax.all_gather(out_weight, both, axis=0, tiled=True)
+    near = lax.all_gather(
+        jnp.concatenate([first_part, out_weight], axis=1), "expert", axis=0, tiled=True
+    )
+    first_width = first_part.shape[1]
+    first_whole = lax.all_gather(near[:, :first_width], "dp", axis=0, tiled=True)
+    w_out = lax.all_gather(near[:, first_width:], "dp", axis=0, tiled=True)
     w_qkv = first_whole[:, :packed_width]
     side = first_whole[:, packed_width:]
     w_router = side[:, :experts]
@@ -185,21 +193,10 @@
     grad_branch = grad_after.astype(jnp.bfloat16)
 
     acc_out = left_dot(attended, grad_branch)
-    acc_router = left_dot(normed_two, grad_logits)
-    out_share = lax.psum_scatter(
-        jnp.concatenate(
-            [
-                acc_out,
-                acc_router,
-                grad_gain_two[:, None],
-                jnp.zeros((model_width, (-(experts + 1)) % 128), jnp.float32),
-            ],
-            axis=1,
-        ).astype(jnp.bfloat16),
-        both,
-        scatter_dimension=0,
-        tiled=True,
-    ).astype(jnp.float32)
+    acc_router = left_dot(grad_logits, normed_two)
+    out_near = lax.psum_scatter(
+        acc_out.astype(jnp.bfloat16), "dp", scatter_dimension=0, tiled=True
+    )
 
     grad_attended = (
         right_dot(grad_branch, w_out)
@@ -233,36 +230,73 @@
     grad_input_norm, grad_gain_one = jax.vjp(rms_scale, inputs, gain_one)[1](grad_normed_one)
     grad_tokens = grad_after + grad_input_norm
     acc_qkv = left_dot(normed_one, grad_packed)
-    qkv_share = lax.psum_scatter(
-        jnp.concatenate(
-            [
-                acc_qkv.astype(jnp.bfloat16),
-                grad_gain_one[:, None].astype(jnp.bfloat16),
-                jnp.zeros((model_width, 127), jnp.bfloat16),
-            ],
-            axis=1,
-        ),
-        both,
-        scatter_dimension=0,
-        tiled=True,
-    ).astype(jnp.float32)
-
-    flat_scores = jnp.sum(grad_scores, axis=0).reshape(head_count, length * length)
-    high = flat_scores.astype(jnp.bfloat16)
-    low = (flat_scores - high.astype(jnp.float32)).astype(jnp.bfloat16)
+    qkv_sum, table_scores = lax.optimization_barrier(
+        (acc_qkv.astype(jnp.bfloat16), jnp.sum(grad_scores, axis=0))
+    )
+    qkv_near = lax.psum_scatter(qkv_sum, "dp", scatter_dimension=0, tiled=True)
+
+    high, low = two_terms(table_scores.reshape(head_count, length * length))
     table_parts = jnp.dot(
         jnp.concatenate([high, low], axis=0), flat_hot, preferred_element_type=jnp.float32
     )
-    acc_table = (table_parts[:head_count] + table_parts[head_count:]).T
-    table_total = lax.psum(acc_table, both)
+    acc_table = (table_parts[:head_count] + table_parts[head_count:]).reshape(-1)
+
+    shard_rows = qkv_weight.shape[0]
+    experts_axis = near.shape[0] // shard_rows
+    small_rows = experts + 3
+    small = jnp.concatenate(
+        [
+            acc_router,
+            grad_gain_one[None],
+            grad_gain_two[None],
+            jnp.pad(acc_table, (0, model_width - acc_table.shape[0]))[None],
+            jnp.zeros(((-small_rows) % 8, model_width), jnp.float32),
+        ],
+        axis=0,
+    )
+    small = jnp.sum(lax.all_gather(small, "dp", axis=0, tiled=False), axis=0)
+    mine = lax.dynamic_slice_in_dim(
+        small[: experts + 2], lax.axis_index("dp") * near.shape[0], near.shape[0], axis=1
+    )
+    mine = mine.T.reshape(experts_axis, shard_rows, experts + 2)
+    table_size = buckets * head_count
+    table_columns = -(-table_size // shard_rows)
+    table_block = jnp.pad(
+        small[experts + 2, :table_size], (0, table_columns * shard_rows - table_size)
+    ).reshape(1, shard_rows, table_columns)
+    extra = jnp.concatenate(
+        [mine, jnp.broadcast_to(table_block, (experts_axis, shard_rows, table_columns))], axis=2
+    )
+    extra_width = extra.shape[2]
+    extra_high, extra_low = two_terms(extra)
+    share = jnp.concatenate(
+        [
+            qkv_near.reshape(experts_axis, shard_rows, packed_width),
+            out_near.reshape(experts_axis, shard_rows, model_width),
+            extra_high,
+            extra_low,
+            jnp.zeros((experts_axis, shard_rows, (-2 * extra_width) % 128), jnp.bfloat16),
+        ],
+        axis=2,
+    )
+    share = lax.all_to_all(share, "expert", split_axis=0, concat_axis=0, tiled=True)
+    share = jnp.sum(share.astype(jnp.float32), axis=0)
+    dense_width = packed_width + model_width
+    extra_sum = (
+        share[:, dense_width : dense_width + extra_width]
+        + share[:, dense_width + extra_width : dense_width + 2 * extra_width]
+    )
+    table_total = (
+        extra_sum[:, experts + 2 :].reshape(-1)[:table_size].reshape(head_count, buckets).T
+    )
     return (
         mixed,
         grad_tokens,
-        qkv_share[:, :packed_width],
-        out_share[:, :model_width],
-        out_share[:, model_width : model_width + experts],
-        qkv_share[:, packed_width],
-        out_share[:, model_width + experts],
+        share[:, :packed_width],
+        share[:, packed_width:dense_width],
+        extra_sum[:, :experts],
+        extra_sum[:, experts],
+        extra_sum[:, experts + 1],
         table_total,
         acc_up[None],
         acc_down[None],

time: 551 us -> 393 us (0.71)
  waiting for transfers between devices: 360 us -> 209 us
    unnamed x8 -> x7, waiting for transfers between devices: 171 us -> 0.12 us
    reduce_scatter x0 -> x2, waiting for transfers between devices: none -> 42.2 us  [the longest x1 42.2 us: shards(): qkv_near = lax.psum_scatter(qkv_sum, 'dp', scatter_dimension=0, tiled=True)]
    psum x1 -> x0, blocking collectives: 37.7 us -> none  [shards(): table_total = lax.psum(acc_table, both)]
    all_to_all x0 -> x1, blocking collectives: none -> 30 us  [shards(): lax.all_to_all(results.reshape(experts, micro_count * capacity, 2 * model...]
    all_gather x2 -> x3, waiting for transfers between devices: 97.9 us -> 73.3 us  [the longest x1 44.2 us: shards(): lax.all_gather(jnp.concatenate([first_part, out_weight], axis=1), 'expert...]
    all_gather x0 -> x1, blocking collectives: none -> 5.61 us  [shards(): small = jnp.sum(lax.all_gather(small, 'dp', axis=0, tiled=False), axis=0)]
    unnamed x100 -> x120, local copies, waits for them, and re-layouts: 14.7 us -> 14.6 us
  transfers between devices with their start and end apart: 7 -> 8, of which waited for: 7 -> 7; matrix products, arithmetic and copies ran while one was open for 9% -> 12% of each run, Pallas kernels for 0% -> 0%
where the time goes in v2:
time: 393 us; the launch traced here: 392 us
  waiting for transfers between devices  209 us (53%)
  blocking collectives  65.8 us (17%)
  matrix products  47.5 us (12%)
  local copies, waits for them, and re-layouts  36 us (9%)
  between operations  15 us (4%)
  other arithmetic  11.9 us (3%)
  starting transfers between devices  6.23 us (2%)
    all_gather x1, waiting for transfers between devices, shards(): lax.all_gather(jnp.concatenate([first_part, out_weight], axis=1), 'expert...  44.2 us
    reduce_scatter x1, waiting for transfers between devices, shards(): results = lax.psum_scatter(results, 'dp', scatter_dimension=0, tiled=True)  43 us
    reduce_scatter x1, waiting for transfers between devices, shards(): qkv_near = lax.psum_scatter(qkv_sum, 'dp', scatter_dimension=0, tiled=True)  42.2 us
    all_gather x1, waiting for transfers between devices, shards(): expert_rows = lax.all_gather(received, 'dp', axis=0, tiled=True)  30.9 us
    all_to_all x1, blocking collectives, shards(): lax.all_to_all(sent.reshape(experts, micro_count * capacity, 2 * model_wi...  30.2 us
    all_to_all x1, blocking collectives, shards(): lax.all_to_all(results.reshape(experts, micro_count * capacity, 2 * model...  30 us
    all_gather x1, waiting for transfers between devices, shards(): lax.all_gather(near[:, :first_width], 'dp', axis=0, tiled=True)  25.5 us
    all_to_all x1, waiting for transfers between devices, shards(): lax.all_to_all(share, 'expert', split_axis=0, concat_axis=0, tiled=True)  19.5 us
  transfers between devices with their start and end apart: 8, of which 7 were waited for; matrix products, arithmetic and copies ran while one was open for 12% of the time, Pallas kernels for 0%

profile of v2, /device:TPU:0, one launch (start us, length us, event | category | flops | bytes accessed | tf_op | source)
XLA Modules:
  0.0 391.5 jit_solution(15954366533563062458)
XLA Ops:
  11.4 44.2 %all-gather.6.cloned.1.call-done = bf16[192,3200]{1,0:T(8,128)(2,1)} async-done(((bf16[24,3200]{1,0:T(8,128)(2,1)}), bf16[192,3200]{1,0:T(8,128)(2,1)}) %all-gather.6.cloned.1.call-update) | async-done | bytes 1228816 | tf_op jit(solution)/shard_map/all_gather | solution.py:87
  55.6 2.2 slice.104
  63.1 25.5 %all-gather.8.cloned.1.call-done = bf16[768,2432]{1,0:T(8,128)(2,1)} async-done(((bf16[192,2432]{1,0:T(8,128)(2,1)}), bf16[768,2432]{1,0:T(8,128)(2,1)}) %all-gather.8.cloned.1.call-update) | async-done | bytes 3735568 | tf_op jit(solution)/shard_map/all_gather | solution.py:91
  91.2 4.1 %convolution_convert_fusion.1 = bf16[256,2304]{1,0:T(8,128)(2,1)} fusion(bf16[768,2432]{1,0:T(8,128)(2,1)} %all-gather.8.cloned.1.call-done, bf16[256,768]{1,0:T(8,128)(2,1)S(1)} %copy-done.4, f32[768]{0:T(1024)S(1)} %get-tuple-element.65, f32[256]{0:T(256)S(1)} %fusion.84), kind=kOutput, calls=%fused_computation.13 | convolution fusion | flops 907345920 | bytes 5115904 | tf_op jit(solution)/shard_map/dot_general | solution.py:126
  102.0 2.2 copy.112
  104.2 3.6 all-gather.10.cloned.1.call-done
  111.9 30.2 %all_to_all.15 = bf16[8,40,1536]{2,1,0:T(8,128)(2,1)} all-to-all(bf16[8,40,1536]{2,1,0:T(8,128)(2,1)S(1)} %bitcast.122), channel_id=1, replica_groups=mesh['dp'=4,'expert'=8] {'expert'}, dimensions={0} | all-to-all | bytes 1966080 | tf_op jit(solution)/shard_map/all_to_all | solution.py:154
  142.4 30.9 %all-gather.12.cloned.1.call-done = bf16[1280,1536]{1,0:T(8,128)(2,1)} async-done(((bf16[320,1536]{1,0:T(8,128)(2,1)}), bf16[1280,1536]{1,0:T(8,128)(2,1)}) %all-gather.12.cloned.1.call-update) | async-done | bytes 3932176 | tf_op jit(solution)/shard_map/all_gather | solution.py:161
  173.4 3.6 fusion.19
  180.5 3.7 fusion.7
  187.2 2.2 pad_maximum_fusion
  189.4 6.1 %copy.129 = bf16[1280,1536]{1,0:T(8,128)(2,1)} copy(bf16[1280,1536]{0,1:T(8,128)(2,1)} %pad_maximum_fusion) | data formatting | bytes 7864320
  195.6 43.0 %reduce-scatter.10.cloned.1.call-done = bf16[320,1536]{1,0:T(8,128)(2,1)} async-done(((bf16[1280,1536]{1,0:T(8,128)(2,1)}), bf16[320,1536]{1,0:T(8,128)(2,1)}) %reduce-scatter.10.cloned.1.call-update) | async-done | bytes 983056 | tf_op jit(solution)/shard_map/reduce_scatter | solution.py:175
  238.6 30.0 %all_to_all.16 = bf16[8,40,1536]{2,1,0:T(8,128)(2,1)S(1)} all-to-all(bf16[8,40,1536]{2,1,0:T(8,128)(2,1)} %bitcast.121), channel_id=1, replica_groups=mesh['dp'=4,'expert'=8] {'expert'}, dimensions={0} | all-to-all | bytes 1966080 | tf_op jit(solution)/shard_map/all_to_all | solution.py:176
  275.8 3.5 fusion.34
  283.7 3.1 convolution_convert_fusion
  287.5 4.3 %fusion.47 = (f32[768]{0:T(1024)S(1)}, f32[256]{0:T(256)S(1)}, f32[256,768]{1,0:T(8,128)}) fusion(bf16[256,768]{1,0:T(8,128)(2,1)S(1)} %copy-done.6, f32[256]{0:T(256)S(1)} %copy-done.45, f32[768]{0:T(1024)S(1)} %copy-done.32, bf16[768,2432]{1,0:T(8,128)(2,1)} %all-gather.8.cloned.1.call-done, bf16[288,8,2,128]{3,2,1,0:T(2,128)(2,1)S(1)} %bitcast.111), kind=kOutput, calls=%fused_computation.74 | convolution fusion | flops 907344896 | bytes 5906432 | tf_op jit(solution)/shard_map/dot_general | solution.py:43
  294.3 5.6 %all-gather = f32[64,768]{1,0:T(8,128)S(1)} all-gather(f32[16,768]{1,0:T(8,128)S(1)} %concatenate.25), channel_id=2, replica_groups=mesh['dp'=4,'expert'=8] {'dp'}, dimensions={0}, use_global_device_ids=true | all-gather | bytes 245760 | tf_op jit(solution)/shard_map/all_gather | solution.py:257
  300.4 42.2 %reduce-scatter.6.cloned.1.call-done = bf16[192,2304]{1,0:T(8,128)(2,1)} async-done(((bf16[768,2304]{1,0:T(8,128)(2,1)}), bf16[192,2304]{1,0:T(8,128)(2,1)}) %reduce-scatter.6.cloned.1.call-update) | async-done | bytes 884752 | tf_op jit(solution)/shard_map/reduce_scatter | solution.py:236
  342.6 3.2 concatenate.27
  345.8 5.5 %all-to-all-start.2 = ((bf16[8,24,3200]{2,1,0:T(8,128)(2,1)}), bf16[8,24,3200]{2,1,0:T(8,128)(2,1)S(1)}, u32[]{:S(2)}, u32[]{:S(2)}) async-start(bf16[8,24,3200]{2,1,0:T(8,128)(2,1)} %concatenate.27), calls=%async_computation.4 | async-start | bytes 2457600 | tf_op jit(solution)/shard_map/all_to_all | solution.py:282
  351.4 5.4 %fusion.22 = f32[1,768,768]{2,1,0:T(8,128)} fusion(bf16[1280,768]{1,0:T(8,128)(2,1)} %copy-done.56, bf16[1280,1536]{1,0:T(8,128)(2,1)} %all-gather.12.cloned.1.call-done), kind=kOutput, calls=%fused_computation.30 | convolution fusion | flops 1509949440 | bytes 6291456 | tf_op jit(solution)/shard_map/dot_general | solution.py:37
  356.9 3.5 fusion.25
  361.5 19.5 %all-to-all-done.2 = bf16[8,24,3200]{2,1,0:T(8,128)(2,1)S(1)} async-done(((bf16[8,24,3200]{2,1,0:T(8,128)(2,1)}), bf16[8,24,3200]{2,1,0:T(8,128)(2,1)S(1)}, u32[]{:S(2)}, u32[]{:S(2)}) %all-to-all-start.2) | async-done | bytes 1228832 | tf_op jit(solution)/shard_map/all_to_all | solution.py:282
  (208 shorter events, 49.1 us)
Async XLA Ops:
  7.2 169.8 %copy-start = (bf16[1,768,768]{2,1,0:T(8,128)(2,1)S(1)}, bf16[1,768,768]{2,1,0:T(8,128)(2,1)}, u32[]{:S(2)}) copy-start(bf16[1,768,768]{2,1,0:T(8,128)(2,1)} %param.24) | copy-start | bytes 3538948
  7.2 50.7 %copy-start.19 = (bf16[16384,32]{0,1:T(8,128)(2,1)S(1)}, bf16[16384,32]{0,1:T(8,128)(2,1)}, u32[]{:S(2)}) copy-start(bf16[16384,32]{0,1:T(8,128)(2,1)} %constant.74.clone) | copy-start | bytes 3145732
  7.2 50.7 %copy-start.48 = (bf16[32,12]{0,1:T(8,128)(2,1)S(1)}, bf16[32,12]{0,1:T(8,128)(2,1)}, u32[]{:S(2)}) copy-start(bf16[32,12]{0,1:T(8,128)(2,1)} %param.22) | copy-start | bytes 2308
  7.2 48.4 %all-gather.6.cloned.1.call-start = ((), (), s32[]{:S(2)}) async-start(), calls=%async_computation.6 | async-start | bytes 1382400 | tf_op jit(solution)/shard_map/all_gather | solution.py:87
  11.3 77.3 %all-gather.8.cloned.1.call-start = ((), (), s32[]{:S(2)}) async-start(), calls=%async_computation.7 | async-start | bytes 4669440 | tf_op jit(solution)/shard_map/all_gather | solution.py:91
  57.8 49.9 %all-gather.10.cloned.1.call-start = ((), (), s32[]{:S(2)}) async-start(), calls=%async_computation.8 | async-start | bytes 1474560 | tf_op jit(solution)/shard_map/all_gather | solution.py:92
  60.0 35.3 %copy-start.46 = (f32[256]{0:T(256)}, f32[256]{0:T(256)S(1)}, u32[]{:S(2)}) copy-start(f32[256]{0:T(256)S(1)} %fusion.51) | copy-start | bytes 3076
  63.0 110.4 %all-gather.12.cloned.1.call-start = ((), (), s32[]{:S(2)}) async-start(), calls=%async_computation.9 | async-start | bytes 4915200 | tf_op jit(solution)/shard_map/all_gather | solution.py:161
  63.1 32.2 %copy-start.44 = (f32[256]{0:T(256)}, f32[256]{0:T(256)S(1)}, u32[]{:S(2)}) copy-start(f32[256]{0:T(256)S(1)} %fusion.84) | copy-start | bytes 3076
  100.6 7.1 %copy-start.5 = (bf16[256,768]{1,0:T(8,128)(2,1)S(1)}, bf16[256,768]{1,0:T(8,128)(2,1)}, u32[]{:S(2)}) copy-start(bf16[256,768]{1,0:T(8,128)(2,1)} %param.14) | copy-start | bytes 1179652
  104.2 5.6 %copy-start.30 = (f32[768]{0:T(1024)S(1)}, f32[768]{0:T(1024)}, u32[]{:S(2)}) copy-start(f32[768]{0:T(1024)} %get-tuple-element.64) | copy-start | bytes 9220
  109.9 32.3 %copy-start.12 = (bf16[256,768]{1,0:T(8,128)(2,1)}, bf16[256,768]{1,0:T(8,128)(2,1)S(1)}, u32[]{:S(2)}) copy-start(bf16[256,768]{1,0:T(8,128)(2,1)S(1)} %multiply_convert_fusion.1) | copy-start | bytes 1179652
  111.3 158.8 %copy-start.37 = (f32[256]{0:T(256)}, f32[256]{0:T(256)S(1)}, u32[]{:S(2)}) copy-start(f32[256]{0:T(256)S(1)} %get-tuple-element.87) | copy-start | bytes 3076
  111.3 158.8 %copy-start.39 = (f32[256]{0:T(256)}, f32[256]{0:T(256)S(1)}, u32[]{:S(2)}) copy-start(f32[256]{0:T(256)S(1)} %fusion.80) | copy-start | bytes 3076
  111.4 158.8 %copy-start.35 = (f32[256]{0:T(256)}, f32[256]{0:T(256)S(1)}, u32[]{:S(2)}) copy-start(f32[256]{0:T(256)S(1)} %select_reduce_fusion.1) | copy-start | bytes 3076
  142.2 96.4 %reduce-scatter.10.cloned.1.call-start = ((), (), s32[]{:S(2)}) async-start(), calls=%async_computation.12 | async-start | bytes 4915200 | tf_op jit(solution)/shard_map/reduce_scatter | solution.py:175
  180.5 5.0 %copy-start.53 = (bf16[1,768,768]{2,1,0:T(8,128)(2,1)S(1)}, bf16[1,768,768]{2,1,0:T(8,128)(2,1)}, u32[]{:S(2)}) copy-start(bf16[1,768,768]{2,1,0:T(8,128)(2,1)} %param.23) | copy-start | bytes 3538948
  195.5 104.8 %reduce-scatter.8.cloned.1.call-start = ((), (), s32[]{:S(2)}) async-start(), calls=%async_computation.11 | async-start | bytes 1474560 | tf_op jit(solution)/shard_map/reduce_scatter | solution.py:197
  274.7 67.9 %reduce-scatter.6.cloned.1.call-start = ((), (), s32[]{:S(2)}) async-start(), calls=%async_computation.10 | async-start | bytes 4423680 | tf_op jit(solution)/shard_map/reduce_scatter | solution.py:236
  287.5 4.4 %copy-start.15 = (f32[12,128,128]{1,2,0:T(8,128)S(1)}, f32[12,128,128]{1,2,0:T(8,128)}, u32[]{:S(2)}) copy-start(f32[12,128,128]{1,2,0:T(8,128)} %get-tuple-element.13) | copy-start | bytes 2359300
  345.8 35.1 %all-to-all-start.2 = ((bf16[8,24,3200]{2,1,0:T(8,128)(2,1)}), bf16[8,24,3200]{2,1,0:T(8,128)(2,1)S(1)}, u32[]{:S(2)}, u32[]{:S(2)}) async-start(bf16[8,24,3200]{2,1,0:T(8,128)(2,1)} %concatenate.27), calls=%async_computation.4 | async-start | bytes 2457600 | tf_op jit(solution)/shard_map/all_to_all | solution.py:282
  351.4 5.5 %copy-start.52 = (bf16[1280,1536]{1,0:T(8,128)(2,1)S(1)}, bf16[1280,1536]{1,0:T(8,128)(2,1)}, u32[]{:S(2)}) copy-start(bf16[1280,1536]{1,0:T(8,128)(2,1)} %all-gather.12.cloned.1.call-done) | copy-start | bytes 11796484
  351.4 5.5 %copy-start.55 = (f32[1280,768]{1,0:T(8,128)S(1)}, f32[1280,768]{1,0:T(8,128)}, u32[]{:S(2)}) copy-start(f32[1280,768]{1,0:T(8,128)} %copy-done.54) | copy-start | bytes 11796484
  360.4 24.3 %copy-start.1 = (bf16[1,768,768]{2,1,0:T(8,128)(2,1)S(1)}, bf16[1,768,768]{2,1,0:T(8,128)(2,1)}, u32[]{:S(2)}) copy-start(bf16[1,768,768]{2,1,0:T(8,128)(2,1)} %param.24) | copy-start | bytes 3538948
  (41 other events, 79.8 us)
Sparse Core Ops, SparseCore 0:
  11.5 44.1 all-gather.5
  57.9 30.6 all-gather.7
  90.2 17.4 all-gather.9
  142.3 30.9 all-gather.11
  195.7 42.8 reduce-scatter.9
  274.8 24.1 reduce-scatter.7
  301.6 40.9 reduce-scatter.5

commit v3 on v2

--- a/solution.py
+++ b/solution.py
@@ -84,9 +84,14 @@
         ],
         axis=1,
     )
-    near = lax.all_gather(
-        jnp.concatenate([first_part, out_weight], axis=1), "expert", axis=0, tiled=True
-    )
+    own = jnp.concatenate([first_part, out_weight], axis=1)
+    near = lax.all_to_all(
+        jnp.broadcast_to(own[None], (lax.axis_size("expert"),) + own.shape),
+        "expert",
+        split_axis=0,
+        concat_axis=0,
+        tiled=True,
+    ).reshape(-1, own.shape[1])
     first_width = first_part.shape[1]
     first_whole = lax.all_gather(near[:, :first_width], "dp", axis=0, tiled=True)
     w_out = lax.all_gather(near[:, first_width:], "dp", axis=0, tiled=True)

time: 393 us -> 383 us (0.975)
  waiting for transfers between devices: 209 us -> 165 us
  blocking collectives: 65.8 us -> 103 us
    all_gather x1 -> x0, waiting for transfers between devices: 44.2 us -> none  [shards(): lax.all_gather(jnp.concatenate([first_part, out_weight], axis=1), 'expert...]
    all_to_all x0 -> x1, blocking collectives: none -> 36.9 us  [shards(): lax.all_to_all(jnp.broadcast_to(own[None], (lax.axis_size('expert'),) + o...]
  transfers between devices with their start and end apart: 8 -> 7, of which waited for: 7 -> 6; matrix products, arithmetic and copies ran while one was open for 12% -> 12% of each run, Pallas kernels for 0% -> 0%
where the time goes in v3:
time: 383 us; the launch traced here: 382 us
  waiting for transfers between devices  165 us (43%)
  blocking collectives  103 us (27%)
  matrix products  46.4 us (12%)
  local copies, waits for them, and re-layouts  34.7 us (9%)
  between operations  14.9 us (4%)
  other arithmetic  11.9 us (3%)
  starting transfers between devices  6.16 us (2%)
    reduce_scatter x1, waiting for transfers between devices, shards(): results = lax.psum_scatter(results, 'dp', scatter_dimension=0, tiled=True)  43 us
    reduce_scatter x1, waiting for transfers between devices, shards(): qkv_near = lax.psum_scatter(qkv_sum, 'dp', scatter_dimension=0, tiled=True)  42.1 us
    all_to_all x1, blocking collectives, shards(): lax.all_to_all(jnp.broadcast_to(own[None], (lax.axis_size('expert'),) + o...  36.9 us
    all_gather x1, waiting for transfers between devices, shards(): expert_rows = lax.all_gather(received, 'dp', axis=0, tiled=True)  30.9 us
    all_to_all x1, blocking collectives, shards(): lax.all_to_all(sent.reshape(experts, micro_count * capacity, 2 * model_wi...  30.3 us
    all_to_all x1, blocking collectives, shards(): lax.all_to_all(results.reshape(experts, micro_count * capacity, 2 * model...  30 us
    all_gather x1, waiting for transfers between devices, shards(): lax.all_gather(near[:, :first_width], 'dp', axis=0, tiled=True)  24.1 us
    all_to_all x1, waiting for transfers between devices, shards(): lax.all_to_all(share, 'expert', split_axis=0, concat_axis=0, tiled=True)  19.5 us
  transfers between devices with their start and end apart: 7, of which 6 were waited for; matrix products, arithmetic and copies ran while one was open for 12% of the time, Pallas kernels for 0%

profile of v3, /device:TPU:0, one launch (start us, length us, event | category | flops | bytes accessed | tf_op | source)
XLA Modules:
  0.0 382.2 jit_solution(15042643620215642675)
XLA Ops:
  10.7 36.9 %all_to_all.20 = bf16[8,24,3200]{2,1,0:T(8,128)(2,1)S(1)} all-to-all(bf16[8,24,3200]{2,1,0:T(8,128)(2,1)S(1)} %broadcast_in_dim.45), channel_id=1, replica_groups=mesh['dp'=4,'expert'=8] {'expert'}, dimensions={0} | all-to-all | bytes 2457600 | tf_op jit(solution)/shard_map/all_to_all | solution.py:88
  50.6 2.3 copy.133
  55.3 24.1 %all-gather.5.cloned.1.call-done = bf16[768,2432]{1,0:T(8,128)(2,1)} async-done(((bf16[192,2432]{1,0:T(8,128)(2,1)}), bf16[768,2432]{1,0:T(8,128)(2,1)}) %all-gather.5.cloned.1.call-update) | async-done | bytes 3735568 | tf_op jit(solution)/shard_map/all_gather | solution.py:96
  81.9 3.1 convolution_convert_fusion.1
  90.7 2.1 copy.135
  92.8 5.7 %all-gather.7.cloned.1.call-done = bf16[768,768]{1,0:T(8,128)(2,1)} async-done(((bf16[192,768]{1,0:T(8,128)(2,1)}), bf16[768,768]{1,0:T(8,128)(2,1)}) %all-gather.7.cloned.1.call-update) | async-done | bytes 1179664 | tf_op jit(solution)/shard_map/all_gather | solution.py:97
  102.7 30.3 %all_to_all.21 = bf16[8,40,1536]{2,1,0:T(8,128)(2,1)} all-to-all(bf16[8,40,1536]{2,1,0:T(8,128)(2,1)S(1)} %bitcast.125), channel_id=1, replica_groups=mesh['dp'=4,'expert'=8] {'expert'}, dimensions={0} | all-to-all | bytes 1966080 | tf_op jit(solution)/shard_map/all_to_all | solution.py:159
  133.2 30.9 %all-gather.9.cloned.1.call-done = bf16[1280,1536]{1,0:T(8,128)(2,1)} async-done(((bf16[320,1536]{1,0:T(8,128)(2,1)}), bf16[1280,1536]{1,0:T(8,128)(2,1)}) %all-gather.9.cloned.1.call-update) | async-done | bytes 3932176 | tf_op jit(solution)/shard_map/all_gather | solution.py:166
  164.2 3.6 fusion.19
  171.3 3.7 fusion.7
  178.0 2.2 pad_maximum_fusion
  180.2 6.2 %copy.152 = bf16[1280,1536]{1,0:T(8,128)(2,1)} copy(bf16[1280,1536]{0,1:T(8,128)(2,1)} %pad_maximum_fusion) | data formatting | bytes 7864320
  186.4 43.0 %reduce-scatter.10.cloned.1.call-done = bf16[320,1536]{1,0:T(8,128)(2,1)} async-done(((bf16[1280,1536]{1,0:T(8,128)(2,1)}), bf16[320,1536]{1,0:T(8,128)(2,1)}) %reduce-scatter.10.cloned.1.call-update) | async-done | bytes 983056 | tf_op jit(solution)/shard_map/reduce_scatter | solution.py:180
  229.4 30.0 %all_to_all.22 = bf16[8,40,1536]{2,1,0:T(8,128)(2,1)S(1)} all-to-all(bf16[8,40,1536]{2,1,0:T(8,128)(2,1)} %bitcast.124), channel_id=1, replica_groups=mesh['dp'=4,'expert'=8] {'expert'}, dimensions={0} | all-to-all | bytes 1966080 | tf_op jit(solution)/shard_map/all_to_all | solution.py:181
  266.6 3.4 fusion.34
  274.5 3.2 convolution_convert_fusion
  278.4 4.3 %fusion.47 = (f32[768]{0:T(1024)S(1)}, f32[256]{0:T(256)S(1)}, f32[256,768]{1,0:T(8,128)}) fusion(bf16[256,768]{1,0:T(8,128)(2,1)S(1)} %copy-done.6, f32[256]{0:T(256)S(1)} %copy-done.45, f32[768]{0:T(1024)S(1)} %copy-done.32, bf16[768,2432]{1,0:T(8,128)(2,1)} %all-gather.5.cloned.1.call-done, bf16[288,8,2,128]{3,2,1,0:T(2,128)(2,1)S(1)} %bitcast.114), kind=kOutput, calls=%fused_computation.74 | convolution fusion | flops 907344896 | bytes 5906432 | tf_op jit(solution)/shard_map/dot_general | solution.py:43
  285.1 5.6 %all-gather = f32[64,768]{1,0:T(8,128)S(1)} all-gather(f32[16,768]{1,0:T(8,128)S(1)} %concatenate.25), channel_id=2, replica_groups=mesh['dp'=4,'expert'=8] {'dp'}, dimensions={0}, use_global_device_ids=true | all-gather | bytes 245760 | tf_op jit(solution)/shard_map/all_gather | solution.py:262
  291.2 42.1 %reduce-scatter.6.cloned.1.call-done = bf16[192,2304]{1,0:T(8,128)(2,1)} async-done(((bf16[768,2304]{1,0:T(8,128)(2,1)}), bf16[192,2304]{1,0:T(8,128)(2,1)}) %reduce-scatter.6.cloned.1.call-update) | async-done | bytes 884752 | tf_op jit(solution)/shard_map/reduce_scatter | solution.py:241
  333.3 3.2 concatenate.27
  336.5 5.5 %all-to-all-start.3 = ((bf16[8,24,3200]{2,1,0:T(8,128)(2,1)}), bf16[8,24,3200]{2,1,0:T(8,128)(2,1)S(1)}, u32[]{:S(2)}, u32[]{:S(2)}) async-start(bf16[8,24,3200]{2,1,0:T(8,128)(2,1)} %concatenate.27), calls=%async_computation.5 | async-start | bytes 2457600 | tf_op jit(solution)/shard_map/all_to_all | solution.py:287
  342.1 5.4 %fusion.22 = f32[1,768,768]{2,1,0:T(8,128)} fusion(bf16[1280,768]{1,0:T(8,128)(2,1)} %copy-done.56, bf16[1280,1536]{1,0:T(8,128)(2,1)} %all-gather.9.cloned.1.call-done), kind=kOutput, calls=%fused_computation.30 | convolution fusion | flops 1509949440 | bytes 6291456 | tf_op jit(solution)/shard_map/dot_general | solution.py:37
  347.5 3.5 fusion.25
  352.2 19.5 %all-to-all-done.3 = bf16[8,24,3200]{2,1,0:T(8,128)(2,1)S(1)} async-done(((bf16[8,24,3200]{2,1,0:T(8,128)(2,1)}), bf16[8,24,3200]{2,1,0:T(8,128)(2,1)S(1)}, u32[]{:S(2)}, u32[]{:S(2)}) %all-to-all-start.3) | async-done | bytes 1228832 | tf_op jit(solution)/shard_map/all_to_all | solution.py:287
  (207 shorter events, 47.5 us)
Async XLA Ops:
  7.2 160.6 %copy-start = (bf16[1,768,768]{2,1,0:T(8,128)(2,1)S(1)}, bf16[1,768,768]{2,1,0:T(8,128)(2,1)}, u32[]{:S(2)}) copy-start(bf16[1,768,768]{2,1,0:T(8,128)(2,1)} %param.24) | copy-start | bytes 3538948
  7.2 72.2 %all-gather.5.cloned.1.call-start = ((), (), s32[]{:S(2)}) async-start(), calls=%async_computation.7 | async-start | bytes 4669440 | tf_op jit(solution)/shard_map/all_gather | solution.py:96
  48.6 49.9 %all-gather.7.cloned.1.call-start = ((), (), s32[]{:S(2)}) async-start(), calls=%async_computation.8 | async-start | bytes 1474560 | tf_op jit(solution)/shard_map/all_gather | solution.py:97
  49.6 4.2 %copy-start.50 = (s32[2,128]{1,0:T(2,128)S(1)}, s32[2,128]{1,0:T(2,128)}, u32[]{:S(2)}) copy-start(s32[2,128]{1,0:T(2,128)} %param.15) | copy-start | bytes 3076
  53.2 28.1 %copy-start.46 = (f32[256]{0:T(256)}, f32[256]{0:T(256)S(1)}, u32[]{:S(2)}) copy-start(f32[256]{0:T(256)S(1)} %fusion.51) | copy-start | bytes 3076
  55.3 108.9 %all-gather.9.cloned.1.call-start = ((), (), s32[]{:S(2)}) async-start(), calls=%async_computation.9 | async-start | bytes 4915200 | tf_op jit(solution)/shard_map/all_gather | solution.py:166
  55.3 26.0 %copy-start.44 = (f32[256]{0:T(256)}, f32[256]{0:T(256)S(1)}, u32[]{:S(2)}) copy-start(f32[256]{0:T(256)S(1)} %fusion.84) | copy-start | bytes 3076
  89.3 9.2 %copy-start.5 = (bf16[256,768]{1,0:T(8,128)(2,1)S(1)}, bf16[256,768]{1,0:T(8,128)(2,1)}, u32[]{:S(2)}) copy-start(bf16[256,768]{1,0:T(8,128)(2,1)} %param.14) | copy-start | bytes 1179652
  92.8 7.7 %copy-start.30 = (f32[768]{0:T(1024)S(1)}, f32[768]{0:T(1024)}, u32[]{:S(2)}) copy-start(f32[768]{0:T(1024)} %get-tuple-element.74) | copy-start | bytes 9220
  98.5 3.6 copy-start.34
  98.5 3.6 copy-start.14
  100.7 32.3 %copy-start.12 = (bf16[256,768]{1,0:T(8,128)(2,1)}, bf16[256,768]{1,0:T(8,128)(2,1)S(1)}, u32[]{:S(2)}) copy-start(bf16[256,768]{1,0:T(8,128)(2,1)S(1)} %multiply_convert_fusion.1) | copy-start | bytes 1179652
  102.1 158.9 %copy-start.37 = (f32[256]{0:T(256)}, f32[256]{0:T(256)S(1)}, u32[]{:S(2)}) copy-start(f32[256]{0:T(256)S(1)} %get-tuple-element.97) | copy-start | bytes 3076
  102.1 158.8 %copy-start.39 = (f32[256]{0:T(256)}, f32[256]{0:T(256)S(1)}, u32[]{:S(2)}) copy-start(f32[256]{0:T(256)S(1)} %fusion.80) | copy-start | bytes 3076
  102.1 158.8 %copy-start.35 = (f32[256]{0:T(256)}, f32[256]{0:T(256)S(1)}, u32[]{:S(2)}) copy-start(f32[256]{0:T(256)S(1)} %select_reduce_fusion.1) | copy-start | bytes 3076
  133.0 96.4 %reduce-scatter.10.cloned.1.call-start = ((), (), s32[]{:S(2)}) async-start(), calls=%async_computation.12 | async-start | bytes 4915200 | tf_op jit(solution)/shard_map/reduce_scatter | solution.py:180
  171.3 5.0 %copy-start.53 = (bf16[1,768,768]{2,1,0:T(8,128)(2,1)S(1)}, bf16[1,768,768]{2,1,0:T(8,128)(2,1)}, u32[]{:S(2)}) copy-start(bf16[1,768,768]{2,1,0:T(8,128)(2,1)} %param.23) | copy-start | bytes 3538948
  186.4 104.8 %reduce-scatter.8.cloned.1.call-start = ((), (), s32[]{:S(2)}) async-start(), calls=%async_computation.11 | async-start | bytes 1474560 | tf_op jit(solution)/shard_map/reduce_scatter | solution.py:202
  265.5 67.8 %reduce-scatter.6.cloned.1.call-start = ((), (), s32[]{:S(2)}) async-start(), calls=%async_computation.10 | async-start | bytes 4423680 | tf_op jit(solution)/shard_map/reduce_scatter | solution.py:241
  278.4 4.3 %copy-start.15 = (f32[12,128,128]{1,2,0:T(8,128)S(1)}, f32[12,128,128]{1,2,0:T(8,128)}, u32[]{:S(2)}) copy-start(f32[12,128,128]{1,2,0:T(8,128)} %get-tuple-element.13) | copy-start | bytes 2359300
  336.5 35.2 %all-to-all-start.3 = ((bf16[8,24,3200]{2,1,0:T(8,128)(2,1)}), bf16[8,24,3200]{2,1,0:T(8,128)(2,1)S(1)}, u32[]{:S(2)}, u32[]{:S(2)}) async-start(bf16[8,24,3200]{2,1,0:T(8,128)(2,1)} %concatenate.27), calls=%async_computation.5 | async-start | bytes 2457600 | tf_op jit(solution)/shard_map/all_to_all | solution.py:287
  342.1 5.5 %copy-start.52 = (bf16[1280,1536]{1,0:T(8,128)(2,1)S(1)}, bf16[1280,1536]{1,0:T(8,128)(2,1)}, u32[]{:S(2)}) copy-start(bf16[1280,1536]{1,0:T(8,128)(2,1)} %all-gather.9.cloned.1.call-done) | copy-start | bytes 11796484
  342.1 5.5 %copy-start.55 = (f32[1280,768]{1,0:T(8,128)S(1)}, f32[1280,768]{1,0:T(8,128)}, u32[]{:S(2)}) copy-start(f32[1280,768]{1,0:T(8,128)} %copy-done.54) | copy-start | bytes 11796484
  351.0 24.4 %copy-start.1 = (bf16[1,768,768]{2,1,0:T(8,128)(2,1)S(1)}, bf16[1,768,768]{2,1,0:T(8,128)(2,1)}, u32[]{:S(2)}) copy-start(bf16[1,768,768]{2,1,0:T(8,128)(2,1)} %param.24) | copy-start | bytes 3538948
  (40 other events, 78.9 us)
Sparse Core Ops, SparseCore 0:
  48.7 30.6 all-gather.4
  81.0 17.4 all-gather.6
  133.1 30.9 all-gather.8
  186.5 42.8 reduce-scatter.9
  265.6 24.2 reduce-scatter.7
  292.3 40.9 reduce-scatter.5
